TPU v7x, 256 devices: a whole 4x4x8 slice. The times are simulated.
256 devices in a mesh: trial: 16 (over z, core), slab: 8 (over y, x_lo), freq: 2 (over x_hi).
Axes of the slice: x: 4 (x_hi: 2, x_lo: 2; x = x_hi * 2 + x_lo), y: 4, z: 8, core: 2. Of those that a mesh axis runs over, the one named last changes fastest.
Arguments:
- orbitals: float32 [16, 32, 64, 128], P('trial', 'slab'), may hold values from -6 to 6
- energies: float32 [16], P('trial'), may hold values from 0 to 1
- potential: float32 [32, 64, 128], P('slab'), may hold values from 0 to 1
- trials: float32 [128, 32, 64, 128], P('trial', 'slab'), may hold values from -6 to 6
- cheb: float32 [2, 4], P('freq'), may hold values from 0.3 to 1
- shifts: float32 [2], P('freq'), may hold values from -0.5 to 0.5
- column_order: int32 [128], replicated, may hold values from 0 to 127, each once
Outputs:
- gram: float32 [128, 128], P(('trial', 'slab'))
Inputs may be any that keep to these rules, and one draw needn't show every extreme that they name: `column_order`: each of 0 to 127 appears once.
All inputs are finite; a program needn't handle non-finite values.
Results may differ from a plain program's by a relative error of at most 0.00024.
Values sent between devices are 32-bit elements; how exact they have to be, the bound alone decides.
No kernel may reach another device: no remote copies, remote signals or barrier semaphores. Data moves between devices by JAX's collectives and lax.ppermute only.
A program may use at most 64 MiB of HBM per device.

v0:
```python
import jax
import jax.numpy as jnp
from jax import lax
from jax.sharding import PartitionSpec as P

KSTEPS = 3


def extended(block, sides, width):
    for axis, dim in sides:
        count = lax.axis_size(axis)
        forward = [(i, i + 1) for i in range(count - 1)]
        backward = [(target, source) for source, target in forward]
        low = lax.ppermute(
            lax.slice_in_dim(block, block.shape[dim] - width, None, axis=dim), axis, forward
        )
        high = lax.ppermute(lax.slice_in_dim(block, 0, width, axis=dim), axis, backward)
        block = jnp.concatenate([low, block, high], axis=dim)
    return block


def lateral(field):
    padded = jnp.pad(field, ((0, 0), (0, 0), (1, 1), (1, 1)))
    total = padded[:, :, 2:, 1:-1] + padded[:, :, :-2, 1:-1]
    return total + padded[:, :, 1:-1, 2:] + padded[:, :, 1:-1, :-2]


def expand(start, operate, coeffs):
    before = start
    now = operate(start)
    response = coeffs[0] * start + coeffs[1] * now
    for order in range(2, KSTEPS + 1):
        after = 2.0 * operate(now) - before
        response = response + coeffs[order] * after
        before, now = (now, after)
    return response


def local(orbitals, energies, potential, trials, cheb, shifts, column_order):
    orb_all, energy_all = (
        lax.all_gather(orbitals, "trial", axis=0, tiled=True),
        lax.all_gather(energies, "trial", axis=0, tiled=True),
    )
    norb = orb_all.shape[0]
    planes = trials.shape[1]
    coeffs = cheb[0]
    shift = shifts[0]
    empty = jnp.zeros(trials.shape, jnp.float32)

    def per_orbital(total, item):
        orbital, energy = item
        coef = potential - energy - shift

        def operate(field):
            padded = extended(field, (("slab", 1),), 1)
            beside = padded[:, 2:] + padded[:, :-2] + lateral(field)
            return (coef[None] * field - 0.5 * beside) / 4.5

        start = orbital[None] * trials
        response = expand(start, operate, coeffs)
        return (total + orbital[None] * response, None)

    density, _ = lax.scan(per_orbital, empty, (orb_all, energy_all))
    spread_rho, spread_trial = (
        lax.all_to_all(density, "trial", split_axis=2, concat_axis=0, tiled=True),
        lax.all_to_all(trials, "trial", split_axis=2, concat_axis=0, tiled=True),
    )
    total_trials = spread_rho.shape[0]
    rho_flat = spread_rho.reshape(total_trials, -1)
    trial_flat = spread_trial.reshape(total_trials, -1)
    columns = jnp.arange(total_trials, dtype=jnp.int32)
    order_table = (column_order[:, None] == columns[None]).astype(jnp.float32)
    rho_sorted = jnp.dot(
        order_table, rho_flat, precision=lax.Precision.HIGHEST, preferred_element_type=jnp.float32
    )
    cells = planes * lax.axis_size("slab") * trials.shape[2] * trials.shape[3]
    factor = 1.0 / jnp.sqrt(jnp.float32(cells * norb))
    picker = (column_order[:, None] == columns[None]).astype(jnp.float32)
    left = jnp.dot(
        picker, trial_flat, precision=lax.Precision.HIGHEST, preferred_element_type=jnp.float32
    )
    product = jnp.dot(
        left, rho_sorted.T, precision=lax.Precision.HIGHEST, preferred_element_type=jnp.float32
    )
    partial_rows = lax.psum_scatter(
        product * factor, ("trial", "slab"), scatter_dimension=0, tiled=True
    )
    return lax.psum(partial_rows, "freq")


def solution(mesh):
    in_specs = (
        P("trial", "slab", None, None),
        P("trial"),
        P("slab", None, None),
        P("trial", "slab", None, None),
        P("freq", None),
        P("freq"),
        P(),
    )
    out_specs = P(("trial", "slab"), None)
    return jax.shard_map(local, mesh=mesh, in_specs=in_specs, out_specs=out_specs, check_vma=False)
```

profile of v0, /device:TPU:1, one launch (start us, length us, event | category | flops | bytes accessed | tf_op | source)
XLA Modules:
  0.0 1790.8 jit_solution(16911157460398661992)
XLA Ops:
  10.2 10.0 all-to-all-start
  23.5 45.6 %all-reduce.3 = f32[16]{0:T(128)S(1)} all-reduce(f32[16]{0:T(128)S(1)} %dynamic-update-slice), channel_id=1, replica_groups=mesh['trial'=16,'slab'=8,'freq'=2] {'trial'}, use_global_device_ids=true, to_apply=%add.3 | all-reduce | flops 16 | bytes 128
  69.2 740.0 %while.14 = (s32[]{:T(128)}, f32[8,4,64,128]{3,2,1,0:T(8,128)}, f32[16,4,64,128]{3,2,1,0:T(8,128)}, f32[4]{0:T(128)S(1)}, f32[8,4,64,128]{3,2,1,0:T(8,128)S(1)},...) while((s32[]{:T(128)}, f32[8,4,64,128]{3,2,1,0:T(8,128)}, ...), condition=%wide.region_1.2_spmd.clone, body=%wide.region_0.1_spmd.clone.sunk | while | flops 12943363 | bytes 27132324 | solution.py:63
  124.5 7.0 collective-permute-done.1
  156.6 7.4 collective-permute-done.5
  175.0 6.9 collective-permute-done.1
  188.0 6.9 collective-permute-done.3
  202.3 7.7 collective-permute-done.5
  220.9 6.9 collective-permute-done.1
  233.7 6.9 collective-permute-done.3
  247.9 7.6 collective-permute-done.5
  266.5 6.9 collective-permute-done.1
  279.4 6.9 collective-permute-done.3
  293.6 7.6 collective-permute-done.5
  312.2 6.9 collective-permute-done.1
  325.1 6.9 collective-permute-done.3
  339.3 7.6 collective-permute-done.5
  357.9 6.9 collective-permute-done.1
  370.8 6.9 collective-permute-done.3
  385.0 7.6 collective-permute-done.5
  403.6 6.9 collective-permute-done.1
  416.5 6.9 collective-permute-done.3
  430.7 7.6 collective-permute-done.5
  449.3 6.9 collective-permute-done.1
  462.2 6.9 collective-permute-done.3
  476.4 7.6 collective-permute-done.5
  495.0 6.9 collective-permute-done.1
  522.1 7.6 collective-permute-done.5
  540.7 6.9 collective-permute-done.1
  553.5 6.9 collective-permute-done.3
  567.8 7.6 collective-permute-done.5
  586.4 6.9 collective-permute-done.1
  599.2 6.9 collective-permute-done.3
  613.5 7.6 collective-permute-done.5
  632.1 6.9 collective-permute-done.1
  644.9 6.9 collective-permute-done.3
  659.2 7.6 collective-permute-done.5
  677.8 6.9 collective-permute-done.1
  704.9 7.6 collective-permute-done.5
  723.5 6.9 collective-permute-done.1
  736.3 6.9 collective-permute-done.3
  750.6 7.6 collective-permute-done.5
  769.2 6.9 collective-permute-done.1
  782.0 6.9 collective-permute-done.3
  796.3 7.6 collective-permute-done.5
  812.0 15.1 all-to-all-start.1
  829.2 25.8 %all-to-all-done.1 = f32[8,4,64,128]{3,0,1,2:T(8,128)S(1)} async-done(((f32[8,4,64,128]{3,0,1,2:T(8,128)}), f32[8,4,64,128]{3,0,1,2:T(8,128)S(1)}, u32[]{:S(2)}, u32[]{:S(2)}) %all-to-all-start.1) | async-done | bytes 1048608 | tf_op jit(solution)/shard_map/all_to_all | solution.py:65
  858.1 918.7 %all-reduce.7.cloned.1.call-done = f32[128,128]{1,0:T(8,128)} async-done(((f32[128,128]{1,0:T(8,128)}), f32[128,128]{1,0:T(8,128)}) %all-reduce.7.cloned.1.call-update) | async-done | bytes 65552
  (359 shorter events, 459.4 us)
Async XLA Ops:
  6.5 62.6 %all-gather.2.cloned.1.call-start = ((), (), s32[]{:S(2)}) async-start(), calls=%async_computation.2 | async-start | bytes 2228224 | tf_op jit(solution)/shard_map/all_gather | solution.py:41
  10.2 801.8 %all-to-all-start = ((f32[8,4,64,128]{3,0,1,2:T(8,128)}), f32[8,4,64,128]{3,0,1,2:T(8,128)}, u32[]{:S(2)}, u32[]{:S(2)}) async-start(f32[8,4,64,128]{3,0,1,2:T(8,128)} %copy.12), calls=%async_computation | async-start | bytes 2097152 | tf_op jit(solution)/shard_map/all_to_all | solution.py:66
  121.2 10.3 collective-permute-start.1
  153.7 10.3 collective-permute-start.5
  171.8 10.2 collective-permute-start.1
  184.7 10.2 collective-permute-start.3
  199.4 10.6 collective-permute-start.5
  217.6 10.2 collective-permute-start.1
  230.4 10.1 collective-permute-start.3
  245.0 10.5 collective-permute-start.5
  263.2 10.1 collective-permute-start.1
  276.1 10.1 collective-permute-start.3
  290.7 10.5 collective-permute-start.5
  308.9 10.1 collective-permute-start.1
  321.8 10.1 collective-permute-start.3
  336.4 10.5 collective-permute-start.5
  354.6 10.1 collective-permute-start.1
  367.5 10.1 collective-permute-start.3
  382.1 10.5 collective-permute-start.5
  400.3 10.1 collective-permute-start.1
  413.2 10.1 collective-permute-start.3
  427.8 10.5 collective-permute-start.5
  446.0 10.1 collective-permute-start.1
  458.9 10.1 collective-permute-start.3
  473.5 10.5 collective-permute-start.5
  491.7 10.1 collective-permute-start.1
  504.6 10.1 collective-permute-start.3
  519.2 10.5 collective-permute-start.5
  537.4 10.1 collective-permute-start.1
  550.3 10.1 collective-permute-start.3
  564.9 10.5 collective-permute-start.5
  583.1 10.1 collective-permute-start.1
  596.0 10.1 collective-permute-start.3
  610.6 10.5 collective-permute-start.5
  628.8 10.1 collective-permute-start.1
  641.7 10.1 collective-permute-start.3
  656.3 10.5 collective-permute-start.5
  674.5 10.1 collective-permute-start.1
  687.4 10.1 collective-permute-start.3
  702.0 10.5 collective-permute-start.5
  720.2 10.1 collective-permute-start.1
  733.1 10.1 collective-permute-start.3
  747.7 10.5 collective-permute-start.5
  765.9 10.1 collective-permute-start.1
  778.8 10.1 collective-permute-start.3
  793.4 10.5 collective-permute-start.5
  812.0 43.0 %all-to-all-start.1 = ((f32[8,4,64,128]{3,0,1,2:T(8,128)}), f32[8,4,64,128]{3,0,1,2:T(8,128)S(1)}, u32[]{:S(2)}, u32[]{:S(2)}) async-start(f32[8,4,64,128]{3,0,1,2:T(8,128)} %copy.15), calls=%async_computation.1 | async-start | bytes 2097152 | tf_op jit(solution)/shard_map/all_to_all | solution.py:65
  827.1 949.7 %all-reduce.7.cloned.1.call-start = ((), (), s32[]{:S(2)}) async-start(), calls=%async_computation.3 | async-start | bytes 131072
  (58 other events, 470.3 us)
Sparse Core Ops, SparseCore 0:
  9.2 53.9 all-gather.1
  857.7 919.1 all-reduce.6
where the time goes:
time: 1800 us; the launch traced here: 1790 us
  waiting for transfers between devices  1330 us (74%)
  starting transfers between devices  197 us (11%)
  other arithmetic  129 us (7%)
  local copies, waits for them, and re-layouts  60.5 us (3%)
  blocking collectives  51.4 us (3%)
    unnamed x3, waiting for transfers between devices  919 us
    ppermute x48, waiting for transfers between devices, extended(): lax.ppermute(lax.slice_in_dim(block, 0, width, axis=dim), axis, backward)  338 us
    ppermute x48, starting transfers between devices, extended(): lax.ppermute(lax.slice_in_dim(block, block.shape[dim] - width, None, axis...  110 us
    add x16, other arithmetic, per_orbital(): return (total + orbital[None] * response, None)  83.7 us
    ppermute x48, starting transfers between devices, extended(): lax.ppermute(lax.slice_in_dim(block, 0, width, axis=dim), axis, backward)  61.8 us
    ppermute x48, waiting for transfers between devices, extended(): lax.ppermute(lax.slice_in_dim(block, block.shape[dim] - width, None, axis...  50 us
    unnamed x1, blocking collectives  45.6 us
  transfers between devices with their start and end apart: 100, of which 98 were waited for; matrix products, arithmetic and copies ran while one was open for 11% of the time, Pallas kernels for 0%

commit v1 on v0

v1 whole, which is shorter than its diff:
```python
import functools
import math

import jax
import jax.numpy as jnp
from jax import lax
from jax.experimental import pallas as pl
from jax.experimental.pallas import tpu as pltpu
from jax.sharding import PartitionSpec as P

AXES = ("trial", "slab", "freq")
HOP = 1.0 / 9.0
HIGHEST = lax.Precision.HIGHEST

TILES = ["e", (1, 3), (0, 3), (0, 0), (0, 1), (0, 2), "o", (1, 0), (1, 1), (1, 2)]
ORB_ROW = {(row, plane): row * 4 + plane for row in range(2) for plane in range(4)}
NTILES = len(TILES)


def tile_span(first, last):
    return first * 8, (last + 1) * 8


PARTS = {
    "ahead": (3, 9, 0, 4),
    "above": (1, 6, 2, 0),
    "below": (1, 9, -2, 0),
    "far": (2, 6, 4, 0),
}


def pieces():
    table = {}
    for name, (first, last, drow, dplane) in {"own": (0, 9, 0, 0), **PARTS}.items():
        orb = (TILES.index("o") - first) * 8
        for k in range(first, last + 1):
            tile = TILES[k]
            if isinstance(tile, tuple):
                key = (tile[0] + drow, tile[1] + dplane)
                table[key] = (name, (k - first) * 8, orb + ORB_ROW[tile])
    return table


def pairs():
    own = [(row, plane) for row in range(2) for plane in range(4)]
    ahead = [(row, plane) for row in range(2) for plane in (4, 5, 6)]
    table = {}

    def near(a, b):
        return abs(a[0] - b[0]) + abs(a[1] - b[1]) <= 3

    def add(a, b):
        if near(a, b):
            table.setdefault(a, []).append(b)

    for n, a in enumerate(own):
        table.setdefault(a, []).append(a)
        for b in own[n + 1 :]:
            add(a, b)
        for b in ahead:
            add(a, b)
        for plane in range(4):
            add(a, (2, plane))
        if a[0] == 1:
            for plane in range(4):
                add(a, (-1, plane))
                add(a, (-2, plane))
                add(a, (4, plane))
    for a in ahead:
        if a[0] == 0:
            others = [(-1, plane) for plane in range(4)] + [(2, 3), (-2, 3)]
        else:
            others = [(2, plane) for plane in range(4)] + [(-1, 3), (3, 3)]
        for b in others:
            add(a, b)
    return table


def kernel(place, cheb_ref, v_ref, order_ref, order2_ref, own, ahead, above, below, far, out_ref):
    refs = {"own": own, "ahead": ahead, "above": above, "below": below, "far": far}
    where = pieces()
    lane = lax.broadcasted_iota(jnp.int32, (8, 128), 1)
    slab, block = place[0], place[1]

    energy = own[:, 0, :]
    a0 = a1 = a2 = a3 = jnp.zeros((16, 128), jnp.float32)
    for w in range(2):
        k0, k1, k2, k3, shift = [cheb_ref[w, n : n + 1, :] for n in range(5)]
        c = (energy + shift) / 4.5
        b0, b1, b2, b3 = k0 - k2, k1 - 3.0 * k3, 2.0 * k2, 4.0 * k3
        a3 = a3 + b3
        a2 = a2 + (b2 - 3.0 * c * b3)
        a1 = a1 + (b1 - 2.0 * c * b2 + 3.0 * c * c * b3)
        a0 = a0 + (b0 - c * b1 + c * c * b2 - c * c * c * b3)
    amp = [a0, a1, a2, a3]

    orb = {}

    def orbital(rp):
        if rp not in orb:
            name, _, row = where[rp]
            orb[rp] = refs[name][:, row, :]
        return orb[rp]

    def trial(rp):
        name, row, _ = where[rp]
        return refs[name][:, row : row + 8, :]

    def turn(x, dz):
        return x if dz == 0 else pltpu.roll(x, dz % 128, x.ndim - 1)

    def inside_row(row):
        y = block * 2 + row
        return ((y >= 0) & (y < 64)).astype(jnp.float32)

    def inside_plane(plane):
        x = slab * 4 + plane
        return ((x >= 0) & (x < 32)).astype(jnp.float32)

    def inside_z(dz):
        return ((lane + dz >= 0) & (lane + dz < 128)).astype(jnp.float32)

    pot = {}

    def potential(row, plane):
        if (row, plane) not in pot:
            at = v_ref[plane + 1, row + 1 : row + 2, :] / 4.5
            pot[(row, plane)] = jnp.broadcast_to(at, (8, 128))
        return pot[(row, plane)]

    ones = jnp.ones((8, 128), jnp.float32)

    def powers(a, b, dz):
        dy, dx = b[0] - a[0], b[1] - a[1]
        step = (dx, dy, dz)
        dist = abs(dx) + abs(dy) + abs(dz)
        ways = math.factorial(dist)
        for s in step:
            ways //= math.factorial(abs(s))
        if dist == 3:
            return None, None, None, -(HOP**3) * ways
        vq = potential(*b) if dist < 3 else None
        vp = turn(potential(*a), dz)
        if dist == 2:
            total = float(ways) * (vp + vq)
            moves = [n for n in range(3) if step[n] != 0]
            for n in moves:
                part = [0, 0, 0]
                part[n] = 1 if step[n] > 0 else -1
                mid = potential(a[0] + part[1], a[1] + part[0])
                total = total + turn(mid, dz - part[2])
            return None, None, HOP**2 * ways, HOP**2 * total
        if dist == 1:
            if dz != 0:
                across = inside_row(a[0] - 1) + inside_row(a[0] + 1) + inside_plane(a[1] - 1) + inside_plane(a[1] + 1)
                along = inside_z(-2 * dz) + inside_z(dz)
            else:
                across = inside_z(1) + inside_z(-1)
                if dy != 0:
                    across = across + inside_plane(a[1] - 1) + inside_plane(a[1] + 1)
                    along = inside_row(a[0] - dy) + inside_row(b[0] + dy)
                else:
                    across = across + inside_row(a[0] - 1) + inside_row(a[0] + 1)
                    along = inside_plane(a[1] - dx) + inside_plane(b[1] + dx)
            walks = (3.0 * across + along + 1.0) * ones
            return None, -HOP, -HOP * (vp + vq), -HOP * (vp * vp + vp * vq + vq * vq) - HOP**3 * walks
        around = [(a[0] - 1, a[1]), (a[0] + 1, a[1]), (a[0], a[1] - 1), (a[0], a[1] + 1)]
        degree = inside_z(1) + inside_z(-1)
        near = inside_z(-1) * turn(vp, 1) + inside_z(1) * turn(vp, -1)
        for row, plane in around:
            here = inside_row(row) * inside_plane(plane)
            degree = degree + here
            near = near + here * potential(row, plane)
        square = vp * vp
        return 1.0, vp, square + HOP**2 * degree, vp * square + HOP**2 * (2.0 * degree * vp + near)

    def coefficient(a, b, dz, left):
        right = orbital(b)
        total = None
        for m, h in enumerate(powers(a, b, dz)):
            if h is None:
                continue
            product = left[m] * right
            term = (product[:8] + product[8:]) * h
            total = term if total is None else total + term
        for s in (4, 2, 1):
            total = total + pltpu.roll(total, s, 0)
        if a == b and dz == 0:
            total = total * 0.5
        if dz != 0:
            total = total * inside_z(-dz)
        return total

    gram = jnp.zeros((128, 128), jnp.float32)
    for a, rights in pairs().items():
        response = None
        for dz in range(-3, 4):
            todo = []
            for b in rights:
                dist = abs(a[0] - b[0]) + abs(a[1] - b[1]) + abs(dz)
                if dist <= 3 and (a != b or dz >= 0):
                    todo.append((b, dist))
            if not todo:
                continue
            moved = turn(orbital(a), dz)
            least = min(dist for _, dist in todo)
            left = [moved * amp[m] if m >= least else None for m in range(4)]
            acc = None
            for b, _ in todo:
                term = coefficient(a, b, dz, left)[None] * trial(b)
                acc = term if acc is None else acc + term
            acc = turn(acc.reshape(128, 128), -dz)
            response = acc if response is None else response + acc
        gram = gram + lax.dot_general(
            trial(a).reshape(128, 128), response, (((1,), (1,)), ((), ())),
            precision=HIGHEST, preferred_element_type=jnp.float32,
        )

    gram = (gram + gram.T) * (1.0 / math.sqrt(32 * 64 * 128 * 16))
    pick = (order_ref[...] == lax.broadcasted_iota(jnp.int32, (128, 128), 0)).astype(jnp.float32)
    pick2 = (order2_ref[...] == lax.broadcasted_iota(jnp.int32, (128, 256), 0)).astype(jnp.float32)
    gram = jnp.dot(gram, pick, precision=HIGHEST, preferred_element_type=jnp.float32)
    out_ref[...] = lax.dot_general(
        pick2, gram, (((0,), (0,)), ((), ())), precision=HIGHEST, preferred_element_type=jnp.float32
    )


def shift_perm(step, dslab):
    perm = []
    for trial in range(16):
        for slab in range(8):
            for freq in range(2):
                block = freq * 16 + trial + step
                other = slab + dslab
                if 0 <= block < 32 and 0 <= other < 8:
                    source = ((block % 16) * 8 + other) * 2 + block // 16
                    perm.append((source, (trial * 8 + slab) * 2 + freq))
    return perm


def local(orbitals, energies, potential, trials, cheb, shifts, column_order):
    trial, slab, freq = (lax.axis_index(a) for a in AXES)
    block = freq * 16 + trial

    padded = jnp.pad(potential, ((0, 0), (1, 7), (0, 0)))
    window = lax.dynamic_slice_in_dim(padded, block * 2, 8, axis=1)
    scalars = jnp.concatenate([cheb[0], shifts, jnp.zeros((3,), jnp.float32)])
    scalars = jnp.broadcast_to(scalars[:, None], (8, 128))
    swap = [
        ((t * 8 + (s + 1) % 8) * 2 + 1 - f, (t * 8 + s) * 2 + f)
        for t in range(16) for s in range(8) for f in range(2)
    ]
    other = lax.dynamic_slice_in_dim(padded, (block ^ 16) * 2, 8, axis=1)
    up = lax.ppermute(jnp.concatenate([other[:2], scalars[None]]), AXES, swap)
    down = lax.ppermute(window[3:4], "slab", [(s, s + 1) for s in range(7)])
    v = jnp.concatenate([down, window, up[:2]])
    both = jnp.stack([scalars, up[2]])

    rows = lax.dynamic_slice_in_dim(trials, freq * 32, 32, axis=2)
    rows = rows.reshape(8, 4, 16, 2, 128).transpose(2, 3, 1, 0, 4)
    orb = lax.dynamic_slice_in_dim(orbitals, freq * 32, 32, axis=2)
    orb = orb.reshape(4, 16, 2, 128).transpose(1, 2, 0, 3).reshape(16, 8, 128)
    energy = jnp.broadcast_to(energies.reshape(1, 1, 1), (16, 8, 128))
    send = [
        energy if t == "e" else orb if t == "o" else rows[:, t[0], t[1]] for t in TILES
    ]
    own = lax.all_to_all(jnp.concatenate(send, axis=1), "trial", split_axis=0, concat_axis=0, tiled=True)

    steps = {"ahead": (0, 1), "above": (1, 0), "below": (-1, 0), "far": (2, 0)}
    halo = {}
    for name, (first, last, _, _) in PARTS.items():
        start, stop = tile_span(first, last)
        halo[name] = lax.ppermute(own[:, start:stop], AXES, shift_perm(*steps[name]))

    place = jnp.stack([slab, block]).astype(jnp.int32)
    smem = pl.BlockSpec(memory_space=pltpu.SMEM)
    vmem = pl.BlockSpec(memory_space=pltpu.VMEM)
    partial = pl.pallas_call(
        kernel,
        out_shape=jax.ShapeDtypeStruct((256, 128), jnp.float32),
        in_specs=[smem] + [vmem] * 9,
        out_specs=vmem,
        compiler_params=pltpu.CompilerParams(vmem_limit_bytes=32 * 1024 * 1024),
    )(
        place, both, v, column_order[None], jnp.repeat(column_order, 2)[None],
        own, halo["ahead"], halo["above"], halo["below"], halo["far"],
    )
    terms = lax.all_to_all(partial, AXES, split_axis=0, concat_axis=0, tiled=True)
    return jnp.sum(terms, axis=0, keepdims=True)


def solution(mesh):
    in_specs = (
        P("trial", "slab", None, None),
        P("trial"),
        P("slab", None, None),
        P("trial", "slab", None, None),
        P("freq", None),
        P("freq"),
        P(),
    )
    out_specs = P(("trial", "slab"), None)
    return jax.shard_map(local, mesh=mesh, in_specs=in_specs, out_specs=out_specs, check_vma=False)
```

time: 1800 us -> 95.2 us (0.05)
  waiting for transfers between devices: 1330 us -> 22.7 us
  starting transfers between devices: 197 us -> 26.4 us
  other arithmetic: 129 us -> 1.55 us
  local copies, waits for them, and re-layouts: 60.5 us -> 15.4 us
  blocking collectives: 51.4 us -> 23.5 us
    unnamed x3 -> x0, waiting for transfers between devices: 919 us -> none
    ppermute x96 -> x6, waiting for transfers between devices: 388 us -> 4.04 us  [the longest x4 4.04 us: local(): lax.ppermute(own[:, start:stop], AXES, shift_perm(*steps[name]))]
    ppermute x96 -> x6, starting transfers between devices: 172 us -> 16.3 us  [the longest x4 7.14 us: local(): lax.ppermute(own[:, start:stop], AXES, shift_perm(*steps[name]))]
    add x16 -> x0, other arithmetic: 83.7 us -> none  [per_orbital(): return (total + orbital[None] * response, None)]
    unnamed x1 -> x0, blocking collectives: 45.6 us -> none
    all_to_all x0 -> x1, blocking collectives: none -> 23.5 us  [local(): lax.all_to_all(partial, AXES, split_axis=0, concat_axis=0, tiled=True)]
    mul x32 -> x0, other arithmetic: 21.1 us -> none  [the longest x16 19.6 us: operate(): return (coef[None] * field - 0.5 * beside) / 4.5]
    slice x65 -> x8, local copies, waits for them, and re-layouts: 26 us -> 5.17 us  [the longest x4 3.17 us: local(): own[:, start:stop]]
  transfers between devices with their start and end apart: 100 -> 7, of which waited for: 98 -> 2; matrix products, arithmetic and copies ran while one was open for 11% -> 6% of each run, Pallas kernels for 0% -> 0%
where the time goes in v1:
time: 95.2 us; the launch traced here: 94.8 us
  starting transfers between devices  26.4 us (28%)
  blocking collectives  23.5 us (25%)
  waiting for transfers between devices  22.7 us (24%)
  local copies, waits for them, and re-layouts  15.4 us (16%)
  Pallas kernels  3.79 us (4%)
  other arithmetic  1.55 us (2%)
  between operations  1.45 us (2%)
    all_to_all x1, blocking collectives, local(): lax.all_to_all(partial, AXES, split_axis=0, concat_axis=0, tiled=True)  23.5 us
    all_to_all x1, waiting for transfers between devices, local(): lax.all_to_all(jnp.concatenate(send, axis=1), 'trial', split_axis=0, conc...  18.6 us
    all_to_all x1, starting transfers between devices, local(): lax.all_to_all(jnp.concatenate(send, axis=1), 'trial', split_axis=0, conc...  10.1 us
    unnamed x22, local copies, waits for them, and re-layouts  8.51 us
    ppermute x4, starting transfers between devices, local(): lax.ppermute(own[:, start:stop], AXES, shift_perm(*steps[name]))  7.14 us
    ppermute x1, starting transfers between devices, local(): up = lax.ppermute(jnp.concatenate([other[:2], scalars[None]]), AXES, swap)  4.92 us
    ppermute x1, starting transfers between devices, local(): down = lax.ppermute(window[3:4], 'slab', [(s, s + 1) for s in range(7)])  4.27 us
    ppermute x4, waiting for transfers between devices, local(): lax.ppermute(own[:, start:stop], AXES, shift_perm(*steps[name]))  4.04 us
  transfers between devices with their start and end apart: 7, of which 2 were waited for; matrix products, arithmetic and copies ran while one was open for 6% of the time, Pallas kernels for 0%

profile of v1, /device:TPU:1, one launch (start us, length us, event | category | flops | bytes accessed | tf_op | source)
XLA Modules:
  0.0 94.8 jit_solution(12607714602170859232)
XLA Ops:
  0.0 0.0 copy-start
  0.0 1.2 %copy-done = f32[8,4,64,128]{3,2,1,0:T(8,128)S(1)} copy-done((f32[8,4,64,128]{3,2,1,0:T(8,128)S(1)}, f32[8,4,64,128]{3,2,1,0:T(8,128)}, u32[]{:S(2)}) %copy-start) | copy-done | bytes 1048600
  1.3 0.3 copy.15
  2.3 0.7 broadcast_dynamic-update-slice_fusion
  2.9 0.6 fusion.7
  3.6 0.6 fusion.6
  4.2 0.6 fusion.5
  4.8 0.7 fusion.4
  5.5 0.6 fusion.3
  6.2 0.6 constant_dynamic-update-slice_fusion
  6.8 0.6 fusion.2
  7.5 0.6 fusion.1
  8.1 0.7 fusion
  8.8 10.1 %all-to-all-start = ((f32[16,80,128]{2,1,0:T(8,128)}), f32[16,80,128]{2,1,0:T(8,128)S(1)}, u32[]{:S(2)}, u32[]{:S(2)}) async-start(f32[16,80,128]{2,1,0:T(8,128)} %fusion), calls=%async_computation | async-start | bytes 1310720 | tf_op jit(solution)/shard_map/all_to_all | solution.py:267
  19.6 0.0 copy-start.5
  19.6 0.6 copy-done.5
  20.2 0.1 pad_maximum_fusion.3
  20.3 18.6 %all-to-all-done.own = f32[16,80,128]{2,1,0:T(8,128)S(1)} async-done(((f32[16,80,128]{2,1,0:T(8,128)}), f32[16,80,128]{2,1,0:T(8,128)S(1)}, u32[]{:S(2)}, u32[]{:S(2)}) %all-to-all-start) | async-done | bytes 655392 | tf_op jit(solution)/shard_map/all_to_all | solution.py:267
  38.9 0.8 slice.76
  39.8 1.9 %collective-permute-start.4 = (f32[16,72,128]{2,1,0:T(8,128)}, f32[16,72,128]{2,1,0:T(8,128)S(1)}, u32[]{:S(2)}, u32[]{:S(2)}) collective-permute-start(f32[16,72,128]{2,1,0:T(8,128)} %slice.76), channel_id=1, source_target_pairs={{240,1},{242,3},{244,5},{246,7},{248,9},{250,11},{252,13},{254,15}... | collective-permute-start | bytes 1769480 | tf_op jit(solution)/shard_map/ppermute | solution.py:273
  41.7 0.1 stack_broadcast_in_dim.2
  41.8 0.6 pad_maximum_fusion.1
  42.4 4.9 %collective-permute-start = (f32[3,8,128]{2,1,0:T(8,128)}, f32[3,8,128]{2,1,0:T(8,128)}, u32[]{:S(2)}, u32[]{:S(2)}) collective-permute-start(f32[3,8,128]{2,1,0:T(8,128)} %pad_maximum_fusion.1), channel_id=1, source_target_pairs={{3,0},{2,1},{5,2},{4,3},{7,4},{6,5},{9,6},{8,7},{11,8},{10,9},{13,... | collective-permute-start | bytes 36872 | tf_op jit(solution)/shard_map/ppermute | solution.py:254
  47.3 0.8 slice.74
  48.1 1.3 %collective-permute-start.2 = (f32[16,56,128]{2,1,0:T(8,128)}, f32[16,56,128]{2,1,0:T(8,128)S(1)}, u32[]{:S(2)}, u32[]{:S(2)}) collective-permute-start(f32[16,56,128]{2,1,0:T(8,128)} %slice.74), channel_id=1, source_target_pairs={{2,0},{3,1},{4,2},{5,3},{6,4},{7,5},{8,6},{9,7},{10,8},{11,9},{12,... | collective-permute-start | bytes 1376264 | tf_op jit(solution)/shard_map/ppermute | solution.py:273
  49.4 0.6 pad_dynamic-slice_fusion.1
  50.0 0.8 slice.75
  50.8 2.7 %collective-permute-start.3 = (f32[16,48,128]{2,1,0:T(8,128)}, f32[16,48,128]{2,1,0:T(8,128)S(1)}, u32[]{:S(2)}, u32[]{:S(2)}) collective-permute-start(f32[16,48,128]{2,1,0:T(8,128)} %slice.75), channel_id=1, source_target_pairs={{16,0},{17,1},{18,2},{19,3},{20,4},{21,5},{22,6},{23,7},{24,8},{25... | collective-permute-start | bytes 1179656 | tf_op jit(solution)/shard_map/ppermute | solution.py:273
  53.5 0.6 pad_dynamic-slice_fusion
  54.1 0.7 slice.77
  54.8 1.3 %collective-permute-start.5 = (f32[16,40,128]{2,1,0:T(8,128)}, f32[16,40,128]{2,1,0:T(8,128)S(1)}, u32[]{:S(2)}, u32[]{:S(2)}) collective-permute-start(f32[16,40,128]{2,1,0:T(8,128)} %slice.77), channel_id=1, source_target_pairs={{32,0},{33,1},{34,2},{35,3},{36,4},{37,5},{38,6},{39,7},{40,8},{41... | collective-permute-start | bytes 983048 | tf_op jit(solution)/shard_map/ppermute | solution.py:273
  56.1 0.0 copy-start.1
  56.1 0.1 pad_add_fusion.place
  56.2 0.6 copy-done.1
  56.7 0.1 broadcast_in_dim.18
  56.8 0.1 broadcast_in_dim_reshape.3.order2_ref
  57.0 0.0 collective-permute-done
  57.0 4.3 %collective-permute-start.1 = (f32[1,8,128]{2,1,0:T(8,128)}, f32[1,8,128]{2,1,0:T(8,128)S(1)}, u32[]{:S(2)}, u32[]{:S(2)}) collective-permute-start(f32[1,8,128]{2,1,0:T(8,128)} %pad_dynamic-slice_fusion), channel_id=1, source_target_pairs={{0,2},{2,4},{4,6},{6,8},{8,10},{10,12},{12,14},{1,3},{3,5},{5,7},{... | collective-permute-start | bytes 12296 | tf_op jit(solution)/shard_map/ppermute | solution.py:255
  61.3 0.7 slice.64
  61.9 0.7 slice.65
  62.6 0.0 collective-permute-done.1
  62.7 4.0 %collective-permute-done.5.far = f32[16,40,128]{2,1,0:T(8,128)S(1)} collective-permute-done((f32[16,40,128]{2,1,0:T(8,128)}, f32[16,40,128]{2,1,0:T(8,128)S(1)}, u32[]{:S(2)}, u32[]{:S(2)}) %collective-permute-start.5) | collective-permute-done | bytes 327712 | tf_op jit(solution)/shard_map/ppermute | solution.py:273
  66.7 0.0 collective-permute-done.3.above
  66.7 0.0 collective-permute-done.2.ahead
  66.7 0.0 collective-permute-done.4.below
  66.7 3.8 %shard_map.73 = f32[256,128]{1,0:T(8,128)S(1)} custom-call(s32[2]{0:T(128)S(1)} %pad_add_fusion.place, f32[2,8,128]{2,1,0:T(8,128)S(1)} %pad_maximum_fusion.2.cheb_ref, f32[7,8,128]{2,1,0:T(8,128)S(1)} %pad_maximum_fusion.v_ref, s32[1,128]{1,0:T(1,128)S(1)} %bitcast.51, s32[1,256]{1,0:T(1,128)S(1)} %broadcast_in_dim_reshape.3.order2_ref, ...), custom_call_target="tpu_custom_call" | custom-call | tf_op jit(solution)/shard_map/pallas_call | solution.py:278
  70.5 23.5 %all_to_all.14 = f32[256,1,128]{2,1,0:T(1,128)S(1)} all-to-all(f32[256,1,128]{2,1,0:T(1,128)S(1)} %bitcast.50), channel_id=1, replica_groups=mesh['trial'=16,'slab'=8,'freq'=2] {'trial','slab','freq'}, dimensions={0} | all-to-all | bytes 262144 | tf_op jit(solution)/shard_map/all_to_all | solution.py:288
  94.0 0.8 reduce_sum.9
  (14 shorter events, 0.2 us)
Async XLA Ops:
  0.0 1.2 %copy-start = (f32[8,4,64,128]{3,2,1,0:T(8,128)S(1)}, f32[8,4,64,128]{3,2,1,0:T(8,128)}, u32[]{:S(2)}) copy-start(f32[8,4,64,128]{3,2,1,0:T(8,128)} %param.10) | copy-start | bytes 3145732
  4.8 1.3 %copy-start.4 = (f32[1,4,64,128]{3,2,1,0:T(8,128)S(1)}, f32[1,4,64,128]{3,2,1,0:T(8,128)}, u32[]{:S(2)}) copy-start(f32[1,4,64,128]{3,2,1,0:T(8,128)} %param.7) | copy-start | bytes 393220
  8.8 11.5 %copy-start.2 = (f32[4,64,128]{2,1,0:T(8,128)S(1)}, f32[4,64,128]{2,1,0:T(8,128)}, u32[]{:S(2)}) copy-start(f32[4,64,128]{2,1,0:T(8,128)} %param.9) | copy-start | bytes 393220
  8.8 30.1 %all-to-all-start = ((f32[16,80,128]{2,1,0:T(8,128)}), f32[16,80,128]{2,1,0:T(8,128)S(1)}, u32[]{:S(2)}, u32[]{:S(2)}) async-start(f32[16,80,128]{2,1,0:T(8,128)} %fusion), calls=%async_computation | async-start | bytes 1310720 | tf_op jit(solution)/shard_map/all_to_all | solution.py:267
  19.6 0.7 copy-start.5
  39.8 26.9 %collective-permute-start.4 = (f32[16,72,128]{2,1,0:T(8,128)}, f32[16,72,128]{2,1,0:T(8,128)S(1)}, u32[]{:S(2)}, u32[]{:S(2)}) collective-permute-start(f32[16,72,128]{2,1,0:T(8,128)} %slice.76), channel_id=1, source_target_pairs={{240,1},{242,3},{244,5},{246,7},{248,9},{250,11},{252,13},{254,15}... | collective-permute-start | bytes 1769480 | tf_op jit(solution)/shard_map/ppermute | solution.py:273
  42.4 14.6 %collective-permute-start = (f32[3,8,128]{2,1,0:T(8,128)}, f32[3,8,128]{2,1,0:T(8,128)}, u32[]{:S(2)}, u32[]{:S(2)}) collective-permute-start(f32[3,8,128]{2,1,0:T(8,128)} %pad_maximum_fusion.1), channel_id=1, source_target_pairs={{3,0},{2,1},{5,2},{4,3},{7,4},{6,5},{9,6},{8,7},{11,8},{10,9},{13,... | collective-permute-start | bytes 36872 | tf_op jit(solution)/shard_map/ppermute | solution.py:254
  48.1 18.6 %collective-permute-start.2 = (f32[16,56,128]{2,1,0:T(8,128)}, f32[16,56,128]{2,1,0:T(8,128)S(1)}, u32[]{:S(2)}, u32[]{:S(2)}) collective-permute-start(f32[16,56,128]{2,1,0:T(8,128)} %slice.74), channel_id=1, source_target_pairs={{2,0},{3,1},{4,2},{5,3},{6,4},{7,5},{8,6},{9,7},{10,8},{11,9},{12,... | collective-permute-start | bytes 1376264 | tf_op jit(solution)/shard_map/ppermute | solution.py:273
  50.8 15.9 %collective-permute-start.3 = (f32[16,48,128]{2,1,0:T(8,128)}, f32[16,48,128]{2,1,0:T(8,128)S(1)}, u32[]{:S(2)}, u32[]{:S(2)}) collective-permute-start(f32[16,48,128]{2,1,0:T(8,128)} %slice.75), channel_id=1, source_target_pairs={{16,0},{17,1},{18,2},{19,3},{20,4},{21,5},{22,6},{23,7},{24,8},{25... | collective-permute-start | bytes 1179656 | tf_op jit(solution)/shard_map/ppermute | solution.py:273
  54.8 11.9 %collective-permute-start.5 = (f32[16,40,128]{2,1,0:T(8,128)}, f32[16,40,128]{2,1,0:T(8,128)S(1)}, u32[]{:S(2)}, u32[]{:S(2)}) collective-permute-start(f32[16,40,128]{2,1,0:T(8,128)} %slice.77), channel_id=1, source_target_pairs={{32,0},{33,1},{34,2},{35,3},{36,4},{37,5},{38,6},{39,7},{40,8},{41... | collective-permute-start | bytes 983048 | tf_op jit(solution)/shard_map/ppermute | solution.py:273
  56.1 0.7 copy-start.1
  57.0 5.7 %collective-permute-start.1 = (f32[1,8,128]{2,1,0:T(8,128)}, f32[1,8,128]{2,1,0:T(8,128)S(1)}, u32[]{:S(2)}, u32[]{:S(2)}) collective-permute-start(f32[1,8,128]{2,1,0:T(8,128)} %pad_dynamic-slice_fusion), channel_id=1, source_target_pairs={{0,2},{2,4},{4,6},{6,8},{8,10},{10,12},{12,14},{1,3},{3,5},{5,7},{... | collective-permute-start | bytes 12296 | tf_op jit(solution)/shard_map/ppermute | solution.py:255
  61.9 0.7 copy-start.3

commit v2 on v1

--- a/solution.py
+++ b/solution.py
@@ -1,4 +1,3 @@
-import functools
 import math
 
 import jax
@@ -12,38 +11,30 @@
 HOP = 1.0 / 9.0
 HIGHEST = lax.Precision.HIGHEST
 
-TILES = ["e", (1, 3), (0, 3), (0, 0), (0, 1), (0, 2), "o", (1, 0), (1, 1), (1, 2)]
-ORB_ROW = {(row, plane): row * 4 + plane for row in range(2) for plane in range(4)}
-NTILES = len(TILES)
-
-
-def tile_span(first, last):
-    return first * 8, (last + 1) * 8
-
-
-PARTS = {
-    "ahead": (3, 9, 0, 4),
-    "above": (1, 6, 2, 0),
-    "below": (1, 9, -2, 0),
-    "far": (2, 6, 4, 0),
-}
+TILES = [(1, 3), (0, 3), (0, 0), (0, 1), (0, 2), "o", (1, 0), (1, 1), (1, 2), "e"]
+ORB = TILES.index("o") * 8
+EXTRA = TILES.index("e") * 8
+OWN = [(row, plane) for row in range(2) for plane in range(4)]
+AHEAD = [(row, plane) for row in range(2) for plane in range(3)]
 
 
 def pieces():
     table = {}
-    for name, (first, last, drow, dplane) in {"own": (0, 9, 0, 0), **PARTS}.items():
-        orb = (TILES.index("o") - first) * 8
-        for k in range(first, last + 1):
-            tile = TILES[k]
-            if isinstance(tile, tuple):
-                key = (tile[0] + drow, tile[1] + dplane)
-                table[key] = (name, (k - first) * 8, orb + ORB_ROW[tile])
+    for k, tile in enumerate(TILES):
+        if isinstance(tile, tuple):
+            row, plane = tile
+            orb = ORB + row * 4 + plane
+            table[tile] = ("own", k * 8, orb)
+            table[(row - 2, plane)] = ("below", k * 8, orb)
+            if k < 6:
+                table[(row + 2, plane)] = ("above", k * 8, orb)
+    for k, (row, plane) in enumerate(AHEAD):
+        table[(row, plane + 4)] = ("ahead", k * 8, 48 + k)
     return table
 
 
 def pairs():
-    own = [(row, plane) for row in range(2) for plane in range(4)]
-    ahead = [(row, plane) for row in range(2) for plane in (4, 5, 6)]
+    ahead = [(row, plane + 4) for row, plane in AHEAD]
     table = {}
 
     def near(a, b):
@@ -53,9 +44,9 @@
         if near(a, b):
             table.setdefault(a, []).append(b)
 
-    for n, a in enumerate(own):
+    for n, a in enumerate(OWN):
         table.setdefault(a, []).append(a)
-        for b in own[n + 1 :]:
+        for b in OWN[n + 1 :]:
             add(a, b)
         for b in ahead:
             add(a, b)
@@ -65,27 +56,82 @@
             for plane in range(4):
                 add(a, (-1, plane))
                 add(a, (-2, plane))
-                add(a, (4, plane))
     for a in ahead:
+        if a[1] == 4:
+            add(a, a)
         if a[0] == 0:
             others = [(-1, plane) for plane in range(4)] + [(2, 3), (-2, 3)]
         else:
             others = [(2, plane) for plane in range(4)] + [(-1, 3), (3, 3)]
         for b in others:
             add(a, b)
+    for plane in range(4):
+        add((-1, plane), (2, plane))
     return table
 
 
-def kernel(place, cheb_ref, v_ref, order_ref, order2_ref, own, ahead, above, below, far, out_ref):
-    refs = {"own": own, "ahead": ahead, "above": above, "below": below, "far": far}
+def pack_kernel(energy, cheb, shift, trials_hbm, orbital_hbm, potential_hbm, out_ref, trials, orbital, potential, sems):
+    trial, slab, freq = (lax.axis_index(a) for a in AXES)
+    half = freq ^ (slab & 1)
+    rows = pl.ds(pl.multiple_of(half * 32, 32), 32)
+    copies = [
+        pltpu.make_async_copy(source, target, sems.at[n])
+        for n, (source, target) in enumerate(
+            [
+                (trials_hbm.at[:, rows, :], trials.reshape(32, 32, 128)),
+                (orbital_hbm.at[:, rows, :], orbital.reshape(4, 32, 128)),
+                (potential_hbm, potential.reshape(4, 64, 128)),
+            ]
+        )
+    ]
+    for copy in copies:
+        copy.start()
+    row_of = lax.broadcasted_iota(jnp.int32, (8, 128), 0)
+    lane = lax.broadcasted_iota(jnp.int32, (8, 128), 1)
+    scalars = jnp.where(row_of == 0, energy[0], 0.0)
+    for n, value in enumerate([cheb[0, 0], cheb[0, 1], cheb[0, 2], cheb[0, 3], shift[0]]):
+        scalars = jnp.where((row_of == n + 2) | ((row_of == 7) & (lane == n)), value, scalars)
+    for copy in copies:
+        copy.wait()
+    for t in range(16):
+        for k, tile in enumerate(TILES):
+            if tile == "o":
+                for row in range(2):
+                    out_ref[t, k * 8 + 4 * row : k * 8 + 4 * row + 4, :] = orbital[pl.ds(2 * t + row, 4, stride=32), :]
+            elif tile == "e":
+                y = jnp.clip(half * 32 + 2 * t + lax.rem(trial, 4) - 1, 0, 63)
+                at = potential[pl.ds(lax.div(trial, 4) * 64 + y, 1), :]
+                out_ref[t, k * 8 : k * 8 + 8, :] = jnp.where(row_of == 1, at, scalars)
+            else:
+                out_ref[t, k * 8 : k * 8 + 8, :] = trials[pl.ds(tile[1] * 32 + 2 * t + tile[0], 8, stride=128), :]
+
+
+def halo_kernel(own, ahead, above):
+    for k, (row, plane) in enumerate(AHEAD):
+        start = TILES.index((row, plane)) * 8
+        ahead[:, k * 8 : k * 8 + 8, :] = own[:, start : start + 8, :]
+        orb = ORB + row * 4 + plane
+        ahead[:, 48 + k : 49 + k, :] = own[:, orb : orb + 1, :]
+    ahead[:, 54:55, :] = own[:, EXTRA + 1 : EXTRA + 2, :]
+    ahead[:, 55:56, :] = own[:, EXTRA + 7 : EXTRA + 8, :]
+    above[...] = own[:, :48, :]
+
+
+def kernel(order_ref, order2_ref, own, ahead, above, below, out_ref):
+    refs = {"own": own, "ahead": ahead, "above": above, "below": below}
     where = pieces()
     lane = lax.broadcasted_iota(jnp.int32, (8, 128), 1)
-    slab, block = place[0], place[1]
-
-    energy = own[:, 0, :]
+    trial_index, slab, freq = (lax.axis_index(a) for a in AXES)
+    block = (freq ^ (slab & 1)) * 16 + trial_index
+
+    energy = own[:, EXTRA, :]
+    theirs = ahead[0, 55:56, :]
     a0 = a1 = a2 = a3 = jnp.zeros((16, 128), jnp.float32)
-    for w in range(2):
-        k0, k1, k2, k3, shift = [cheb_ref[w, n : n + 1, :] for n in range(5)]
+    for scalars in (
+        [own[0, EXTRA + n : EXTRA + n + 1, :] for n in range(2, 7)],
+        [jnp.broadcast_to(theirs[:, n : n + 1], (1, 128)) for n in range(5)],
+    ):
+        k0, k1, k2, k3, shift = scalars
         c = (energy + shift) / 4.5
         b0, b1, b2, b3 = k0 - k2, k1 - 3.0 * k3, 2.0 * k2, 4.0 * k3
         a3 = a3 + b3
@@ -100,6 +146,8 @@
         if rp not in orb:
             name, _, row = where[rp]
             orb[rp] = refs[name][:, row, :]
+            if name == "ahead":
+                orb[rp] = orb[rp] * inside_plane(4)
         return orb[rp]
 
     def trial(rp):
@@ -124,8 +172,9 @@
 
     def potential(row, plane):
         if (row, plane) not in pot:
-            at = v_ref[plane + 1, row + 1 : row + 2, :] / 4.5
-            pot[(row, plane)] = jnp.broadcast_to(at, (8, 128))
+            ref, at = (own, EXTRA + 1) if plane < 4 else (ahead, 54)
+            source = plane % 4 * 4 + row + 1
+            pot[(row, plane)] = jnp.broadcast_to(ref[source, at : at + 1, :] / 4.5, (8, 128))
         return pot[(row, plane)]
 
     ones = jnp.ones((8, 128), jnp.float32)
@@ -164,13 +213,16 @@
                     along = inside_plane(a[1] - dx) + inside_plane(b[1] + dx)
             walks = (3.0 * across + along + 1.0) * ones
             return None, -HOP, -HOP * (vp + vq), -HOP * (vp * vp + vp * vq + vq * vq) - HOP**3 * walks
+        if a[1] == 4:
+            return None, None, None, HOP**2 * potential(a[0], 3)
         around = [(a[0] - 1, a[1]), (a[0] + 1, a[1]), (a[0], a[1] - 1), (a[0], a[1] + 1)]
         degree = inside_z(1) + inside_z(-1)
         near = inside_z(-1) * turn(vp, 1) + inside_z(1) * turn(vp, -1)
         for row, plane in around:
             here = inside_row(row) * inside_plane(plane)
             degree = degree + here
-            near = near + here * potential(row, plane)
+            if plane >= 0:
+                near = near + here * potential(row, plane)
         square = vp * vp
         return 1.0, vp, square + HOP**2 * degree, vp * square + HOP**2 * (2.0 * degree * vp + near)
 
@@ -198,7 +250,7 @@
             todo = []
             for b in rights:
                 dist = abs(a[0] - b[0]) + abs(a[1] - b[1]) + abs(dz)
-                if dist <= 3 and (a != b or dz >= 0):
+                if dist <= 3 and (a != b or dz == 0 or (dz > 0 and a[1] < 4)):
                     todo.append((b, dist))
             if not todo:
                 continue
@@ -225,66 +277,60 @@
     )
 
 
+def device(block, slab):
+    return ((block % 16) * 8 + slab) * 2 + ((block // 16) ^ (slab & 1))
+
+
 def shift_perm(step, dslab):
-    perm = []
-    for trial in range(16):
-        for slab in range(8):
-            for freq in range(2):
-                block = freq * 16 + trial + step
-                other = slab + dslab
-                if 0 <= block < 32 and 0 <= other < 8:
-                    source = ((block % 16) * 8 + other) * 2 + block // 16
-                    perm.append((source, (trial * 8 + slab) * 2 + freq))
-    return perm
+    return [
+        (device(block + step, (slab + dslab) % 8), device(block, slab))
+        for block in range(32)
+        for slab in range(8)
+        if 0 <= block + step < 32
+    ]
 
 
 def local(orbitals, energies, potential, trials, cheb, shifts, column_order):
-    trial, slab, freq = (lax.axis_index(a) for a in AXES)
-    block = freq * 16 + trial
-
-    padded = jnp.pad(potential, ((0, 0), (1, 7), (0, 0)))
-    window = lax.dynamic_slice_in_dim(padded, block * 2, 8, axis=1)
-    scalars = jnp.concatenate([cheb[0], shifts, jnp.zeros((3,), jnp.float32)])
-    scalars = jnp.broadcast_to(scalars[:, None], (8, 128))
-    swap = [
-        ((t * 8 + (s + 1) % 8) * 2 + 1 - f, (t * 8 + s) * 2 + f)
-        for t in range(16) for s in range(8) for f in range(2)
-    ]
-    other = lax.dynamic_slice_in_dim(padded, (block ^ 16) * 2, 8, axis=1)
-    up = lax.ppermute(jnp.concatenate([other[:2], scalars[None]]), AXES, swap)
-    down = lax.ppermute(window[3:4], "slab", [(s, s + 1) for s in range(7)])
-    v = jnp.concatenate([down, window, up[:2]])
-    both = jnp.stack([scalars, up[2]])
-
-    rows = lax.dynamic_slice_in_dim(trials, freq * 32, 32, axis=2)
-    rows = rows.reshape(8, 4, 16, 2, 128).transpose(2, 3, 1, 0, 4)
-    orb = lax.dynamic_slice_in_dim(orbitals, freq * 32, 32, axis=2)
-    orb = orb.reshape(4, 16, 2, 128).transpose(1, 2, 0, 3).reshape(16, 8, 128)
-    energy = jnp.broadcast_to(energies.reshape(1, 1, 1), (16, 8, 128))
-    send = [
-        energy if t == "e" else orb if t == "o" else rows[:, t[0], t[1]] for t in TILES
-    ]
-    own = lax.all_to_all(jnp.concatenate(send, axis=1), "trial", split_axis=0, concat_axis=0, tiled=True)
-
-    steps = {"ahead": (0, 1), "above": (1, 0), "below": (-1, 0), "far": (2, 0)}
-    halo = {}
-    for name, (first, last, _, _) in PARTS.items():
-        start, stop = tile_span(first, last)
-        halo[name] = lax.ppermute(own[:, start:stop], AXES, shift_perm(*steps[name]))
-
-    place = jnp.stack([slab, block]).astype(jnp.int32)
     smem = pl.BlockSpec(memory_space=pltpu.SMEM)
     vmem = pl.BlockSpec(memory_space=pltpu.VMEM)
+    params = pltpu.CompilerParams(vmem_limit_bytes=32 * 1024 * 1024)
+
+    def shape(rows, lead=(16,)):
+        return jax.ShapeDtypeStruct((*lead, rows, 128), jnp.float32)
+
+    send = pl.pallas_call(
+        pack_kernel,
+        out_shape=shape(len(TILES) * 8),
+        in_specs=[smem] * 3 + [pl.BlockSpec(memory_space=pltpu.HBM)] * 3,
+        out_specs=vmem,
+        scratch_shapes=[
+            pltpu.VMEM((1024, 128), jnp.float32),
+            pltpu.VMEM((128, 128), jnp.float32),
+            pltpu.VMEM((256, 128), jnp.float32),
+            pltpu.SemaphoreType.DMA((3,)),
+        ],
+        compiler_params=pltpu.CompilerParams(vmem_limit_bytes=60 * 1024 * 1024),
+    )(energies, cheb, shifts, trials.reshape(32, 64, 128), orbitals[0], potential)
+    own = lax.all_to_all(send, "trial", split_axis=0, concat_axis=0, tiled=True)
+
+    ahead, above = pl.pallas_call(
+        halo_kernel,
+        out_shape=[shape(56), shape(48)],
+        in_specs=[vmem],
+        out_specs=[vmem] * 2,
+        compiler_params=params,
+    )(own)
+    ahead = lax.ppermute(ahead, AXES, shift_perm(0, 1))
+    below = lax.ppermute(own, AXES, shift_perm(-1, 0))
+    above = lax.ppermute(above, AXES, shift_perm(1, 0))
+
     partial = pl.pallas_call(
         kernel,
-        out_shape=jax.ShapeDtypeStruct((256, 128), jnp.float32),
-        in_specs=[smem] + [vmem] * 9,
+        out_shape=shape(256, ()),
+        in_specs=[vmem] * 6,
         out_specs=vmem,
-        compiler_params=pltpu.CompilerParams(vmem_limit_bytes=32 * 1024 * 1024),
-    )(
-        place, both, v, column_order[None], jnp.repeat(column_order, 2)[None],
-        own, halo["ahead"], halo["above"], halo["below"], halo["far"],
-    )
+        compiler_params=params,
+    )(column_order[None], jnp.repeat(column_order, 2)[None], own, ahead, above, below)
     terms = lax.all_to_all(partial, AXES, split_axis=0, concat_axis=0, tiled=True)
     return jnp.sum(terms, axis=0, keepdims=True)
 

time: 95.2 us -> 82 us (0.86)
  blocking collectives: 23.5 us -> 56.5 us
  starting transfers between devices: 26.4 us -> 9.63 us
  waiting for transfers between devices: 22.7 us -> 6.45 us
  local copies, waits for them, and re-layouts: 15.4 us -> 0.23 us
  Pallas kernels: 3.79 us -> 6.72 us
    all_to_all x0 -> x1, blocking collectives: none -> 30.2 us  [local(): own = lax.all_to_all(send, 'trial', split_axis=0, concat_axis=0, tiled=True)]
    all_to_all x1 -> x0, waiting for transfers between devices: 18.6 us -> none  [local(): lax.all_to_all(jnp.concatenate(send, axis=1), 'trial', split_axis=0, conc...]
    all_to_all x1 -> x0, starting transfers between devices: 10.1 us -> none  [local(): lax.all_to_all(jnp.concatenate(send, axis=1), 'trial', split_axis=0, conc...]
    unnamed x22 -> x2, local copies, waits for them, and re-layouts: 8.51 us -> 0.01 us
    ppermute x6 -> x3, starting transfers between devices: 16.3 us -> 9.63 us  [the longest x1 5.01 us: local(): ahead = lax.ppermute(ahead, AXES, shift_perm(0, 1))]
    slice x8 -> x0, local copies, waits for them, and re-layouts: 5.17 us -> none  [the longest x4 3.17 us: local(): own[:, start:stop]]
    pallas_call x1 -> x3, Pallas kernels: 3.79 us -> 6.72 us  [the longest x1 3.67 us: local(): pl.pallas_call(kernel, out_shape=shape(256, ()), in_specs=[vmem] * 6, out...]
    all_to_all x1, blocking collectives: 23.5 us -> 26.3 us  [local(): lax.all_to_all(partial, AXES, split_axis=0, concat_axis=0, tiled=True)]
  transfers between devices with their start and end apart: 7 -> 3, of which waited for: 2 -> 2; matrix products, arithmetic and copies ran while one was open for 6% -> 0% of each run, Pallas kernels for 0% -> 0%
where the time goes in v2:
time: 82 us; the launch traced here: 81.7 us
  blocking collectives  56.5 us (69%)
  starting transfers between devices  9.63 us (12%)
  Pallas kernels  6.72 us (8%)
  waiting for transfers between devices  6.45 us (8%)
  between operations  1.36 us (2%)
    all_to_all x1, blocking collectives, local(): own = lax.all_to_all(send, 'trial', split_axis=0, concat_axis=0, tiled=True)  30.2 us
    all_to_all x1, blocking collectives, local(): lax.all_to_all(partial, AXES, split_axis=0, concat_axis=0, tiled=True)  26.3 us
    ppermute x1, waiting for transfers between devices, local(): above = lax.ppermute(above, AXES, shift_perm(1, 0))  6.15 us
    ppermute x1, starting transfers between devices, local(): ahead = lax.ppermute(ahead, AXES, shift_perm(0, 1))  5.01 us
    pallas_call x1, Pallas kernels, local(): pl.pallas_call(kernel, out_shape=shape(256, ()), in_specs=[vmem] * 6, out...  3.67 us
    pallas_call x1, Pallas kernels, local(): pl.pallas_call(pack_kernel, out_shape=shape(len(TILES) * 8), in_specs=[sm...  2.97 us
    ppermute x1, starting transfers between devices, local(): above = lax.ppermute(above, AXES, shift_perm(1, 0))  2.69 us
    ppermute x1, starting transfers between devices, local(): below = lax.ppermute(own, AXES, shift_perm(-1, 0))  1.93 us
  transfers between devices with their start and end apart: 3, of which 2 were waited for; matrix products, arithmetic and copies ran while one was open for 0% of the time, Pallas kernels for 0%

profile of v2, /device:TPU:1, one launch (start us, length us, event | category | flops | bytes accessed | tf_op | source)
XLA Modules:
  0.0 81.7 jit_solution(7554464675747915789)
XLA Ops:
  1.3 3.0 %shard_map.73 = f32[16,80,128]{2,1,0:T(8,128)} custom-call(f32[1]{0:T(128)S(6)} %copy.9.energy, f32[1,4]{1,0:T(1,128)} %cheb.1, f32[1]{0:T(128)S(6)} %copy.10.shift, f32[32,64,128]{2,1,0:T(8,128)} %bitcast.9, f32[4,64,128]{2,1,0:T(8,128)} %bitcast.10, f32[4,64,128]{2,1,0:T(8,128)} %potential_hbm.1), custom_call_target="tpu_custom_call" | custom-call | tf_op jit(solution)/shard_map/pallas_call | solution.py:301
  4.3 30.2 %all_to_all.14.own = f32[16,80,128]{2,1,0:T(8,128)S(1)} all-to-all(f32[16,80,128]{2,1,0:T(8,128)} %shard_map.73), channel_id=1, replica_groups=mesh['trial'=16,'slab'=8,'freq'=2] {'trial'}, dimensions={0} | all-to-all | bytes 1310720 | tf_op jit(solution)/shard_map/all_to_all | solution.py:314
  34.5 1.9 %collective-permute-start.2 = (f32[16,80,128]{2,1,0:T(8,128)S(1)}, f32[16,80,128]{2,1,0:T(8,128)S(1)}, u32[]{:S(2)}, u32[]{:S(2)}) collective-permute-start(f32[16,80,128]{2,1,0:T(8,128)S(1)} %all_to_all.14.own), channel_id=1, source_target_pairs={{0,16},{3,19},{4,20},{7,23},{8,24},{11,27},{12,28},{15,31},{16,32}... | collective-permute-start | bytes 1966088 | tf_op jit(solution)/shard_map/ppermute | solution.py:324
  36.4 0.1 shard_map.74
  36.5 0.0 copy-start
  36.5 5.0 %collective-permute-start = (f32[16,56,128]{2,1,0:T(8,128)S(1)}, f32[16,56,128]{2,1,0:T(8,128)S(1)}, u32[]{:S(2)}, u32[]{:S(2)}) collective-permute-start(f32[16,56,128]{2,1,0:T(8,128)S(1)} %get-tuple-element.7), channel_id=1, source_target_pairs={{3,0},{4,3},{7,4},{8,7},{11,8},{12,11},{15,12},{0,15},{19,16},{20,... | collective-permute-start | bytes 1376264 | tf_op jit(solution)/shard_map/ppermute | solution.py:323
  41.5 2.7 %collective-permute-start.1 = (f32[16,48,128]{2,1,0:T(8,128)S(1)}, f32[16,48,128]{2,1,0:T(8,128)S(1)}, u32[]{:S(2)}, u32[]{:S(2)}) collective-permute-start(f32[16,48,128]{2,1,0:T(8,128)S(1)} %get-tuple-element.8), channel_id=1, source_target_pairs={{16,0},{19,3},{20,4},{23,7},{24,8},{27,11},{28,12},{31,15},{32,16}... | collective-permute-start | bytes 1179656 | tf_op jit(solution)/shard_map/ppermute | solution.py:325
  44.2 0.0 copy-done
  44.2 0.1 broadcast_in_dim.10
  44.3 0.1 broadcast_in_dim_reshape.3.order2_ref
  44.5 6.2 %collective-permute-done.1.above = f32[16,48,128]{2,1,0:T(8,128)S(1)} collective-permute-done((f32[16,48,128]{2,1,0:T(8,128)S(1)}, f32[16,48,128]{2,1,0:T(8,128)S(1)}, u32[]{:S(2)}, u32[]{:S(2)}) %collective-permute-start.1) | collective-permute-done | bytes 393248 | tf_op jit(solution)/shard_map/ppermute | solution.py:325
  50.6 0.3 collective-permute-done.ahead
  50.9 0.0 collective-permute-done.2.below
  50.9 3.7 %shard_map.75 = f32[256,128]{1,0:T(8,128)S(1)} custom-call(s32[1,128]{1,0:T(1,128)S(1)} %bitcast.8, s32[1,256]{1,0:T(1,128)S(1)} %broadcast_in_dim_reshape.3.order2_ref, f32[16,80,128]{2,1,0:T(8,128)S(1)} %all_to_all.14.own, f32[16,56,128]{2,1,0:T(8,128)S(1)} %collective-permute-done.ahead, f32[16,48,128]{2,1,0:T(8,128)S(1)} %collective-permute-done.1.above, ...), custom_call_target="tpu_custom_call" | custom-call | tf_op jit(solution)/shard_map/pallas_call | solution.py:327
  54.6 26.3 %all_to_all.15 = f32[256,1,128]{2,1,0:T(1,128)S(1)} all-to-all(f32[256,1,128]{2,1,0:T(1,128)S(1)} %bitcast.7), channel_id=1, replica_groups=mesh['trial'=16,'slab'=8,'freq'=2] {'trial','slab','freq'}, dimensions={0} | all-to-all | bytes 262144 | tf_op jit(solution)/shard_map/all_to_all | solution.py:334
  80.9 0.8 reduce_sum.9
Async XLA Ops:
  34.5 16.4 %collective-permute-start.2 = (f32[16,80,128]{2,1,0:T(8,128)S(1)}, f32[16,80,128]{2,1,0:T(8,128)S(1)}, u32[]{:S(2)}, u32[]{:S(2)}) collective-permute-start(f32[16,80,128]{2,1,0:T(8,128)S(1)} %all_to_all.14.own), channel_id=1, source_target_pairs={{0,16},{3,19},{4,20},{7,23},{8,24},{11,27},{12,28},{15,31},{16,32}... | collective-permute-start | bytes 1966088 | tf_op jit(solution)/shard_map/ppermute | solution.py:324
  36.5 7.7 %copy-start = (s32[128]{0:T(128)S(1)}, s32[128]{0:T(128)}, u32[]{:S(2)}) copy-start(s32[128]{0:T(128)} %param.13) | copy-start | bytes 1540
  36.5 14.4 %collective-permute-start = (f32[16,56,128]{2,1,0:T(8,128)S(1)}, f32[16,56,128]{2,1,0:T(8,128)S(1)}, u32[]{:S(2)}, u32[]{:S(2)}) collective-permute-start(f32[16,56,128]{2,1,0:T(8,128)S(1)} %get-tuple-element.7), channel_id=1, source_target_pairs={{3,0},{4,3},{7,4},{8,7},{11,8},{12,11},{15,12},{0,15},{19,16},{20,... | collective-permute-start | bytes 1376264 | tf_op jit(solution)/shard_map/ppermute | solution.py:323
  41.5 9.1 %collective-permute-start.1 = (f32[16,48,128]{2,1,0:T(8,128)S(1)}, f32[16,48,128]{2,1,0:T(8,128)S(1)}, u32[]{:S(2)}, u32[]{:S(2)}) collective-permute-start(f32[16,48,128]{2,1,0:T(8,128)S(1)} %get-tuple-element.8), channel_id=1, source_target_pairs={{16,0},{19,3},{20,4},{23,7},{24,8},{27,11},{28,12},{31,15},{32,16}... | collective-permute-start | bytes 1179656 | tf_op jit(solution)/shard_map/ppermute | solution.py:325

commit v3 on v2

--- a/solution.py
+++ b/solution.py
@@ -11,25 +11,26 @@
 HOP = 1.0 / 9.0
 HIGHEST = lax.Precision.HIGHEST
 
-TILES = [(1, 3), (0, 3), (0, 0), (0, 1), (0, 2), "o", (1, 0), (1, 1), (1, 2), "e"]
+TILES = [(0, 0), (0, 1), (0, 2), (0, 3), (1, 0), (1, 1), (1, 2), (1, 3), "o", "e"]
 ORB = TILES.index("o") * 8
 EXTRA = TILES.index("e") * 8
 OWN = [(row, plane) for row in range(2) for plane in range(4)]
-AHEAD = [(row, plane) for row in range(2) for plane in range(3)]
+PARTS = {
+    "ahead": ([(row, plane) for row in range(2) for plane in range(3)], 0, 4),
+    "above": ([(0, 0), (0, 1), (0, 2), (0, 3), (1, 0), (1, 1), (1, 3)], 2, 0),
+    "below": ([(1, 0), (1, 1), (1, 2), (1, 3), (0, 2), (0, 3)], -2, 0),
+}
+AHEAD = PARTS["ahead"][0]
 
 
 def pieces():
     table = {}
-    for k, tile in enumerate(TILES):
-        if isinstance(tile, tuple):
-            row, plane = tile
-            orb = ORB + row * 4 + plane
-            table[tile] = ("own", k * 8, orb)
-            table[(row - 2, plane)] = ("below", k * 8, orb)
-            if k < 6:
-                table[(row + 2, plane)] = ("above", k * 8, orb)
-    for k, (row, plane) in enumerate(AHEAD):
-        table[(row, plane + 4)] = ("ahead", k * 8, 48 + k)
+    for rp in OWN:
+        table[rp] = ("own", TILES.index(rp) * 8, ORB + OWN.index(rp))
+    for name, (taken, drow, dplane) in PARTS.items():
+        for k, rp in enumerate(taken):
+            orb = k if name == "ahead" else OWN.index(rp)
+            table[(rp[0] + drow, rp[1] + dplane)] = (name, k * 8, len(taken) * 8 + orb)
     return table
 
 
@@ -55,7 +56,10 @@
         if a[0] == 1:
             for plane in range(4):
                 add(a, (-1, plane))
-                add(a, (-2, plane))
+        if a in ((0, 0), (0, 1), (0, 3)):
+            add(a, (3, a[1]))
+        if a == (1, 2):
+            add(a, (-2, 2))
     for a in ahead:
         if a[1] == 4:
             add(a, a)
@@ -70,9 +74,13 @@
     return table
 
 
-def pack_kernel(energy, cheb, shift, trials_hbm, orbital_hbm, potential_hbm, out_ref, trials, orbital, potential, sems):
+def half_of(slab, freq):
+    return freq ^ (((slab + 1) // 2) & 1)
+
+
+def pack_kernel(energy, cheb, shift, trials_hbm, orbital_hbm, potential_hbm, out_ref, scalars_ref, trials, orbital, potential, sems):
     trial, slab, freq = (lax.axis_index(a) for a in AXES)
-    half = freq ^ (slab & 1)
+    half = freq ^ (lax.div(slab + 1, 2) & 1)
     rows = pl.ds(pl.multiple_of(half * 32, 32), 32)
     copies = [
         pltpu.make_async_copy(source, target, sems.at[n])
@@ -87,10 +95,10 @@
     for copy in copies:
         copy.start()
     row_of = lax.broadcasted_iota(jnp.int32, (8, 128), 0)
-    lane = lax.broadcasted_iota(jnp.int32, (8, 128), 1)
     scalars = jnp.where(row_of == 0, energy[0], 0.0)
     for n, value in enumerate([cheb[0, 0], cheb[0, 1], cheb[0, 2], cheb[0, 3], shift[0]]):
-        scalars = jnp.where((row_of == n + 2) | ((row_of == 7) & (lane == n)), value, scalars)
+        scalars = jnp.where(row_of == n + 2, value, scalars)
+    scalars_ref[...] = scalars
     for copy in copies:
         copy.wait()
     for t in range(16):
@@ -106,32 +114,31 @@
                 out_ref[t, k * 8 : k * 8 + 8, :] = trials[pl.ds(tile[1] * 32 + 2 * t + tile[0], 8, stride=128), :]
 
 
-def halo_kernel(own, ahead, above):
-    for k, (row, plane) in enumerate(AHEAD):
-        start = TILES.index((row, plane)) * 8
-        ahead[:, k * 8 : k * 8 + 8, :] = own[:, start : start + 8, :]
-        orb = ORB + row * 4 + plane
-        ahead[:, 48 + k : 49 + k, :] = own[:, orb : orb + 1, :]
-    ahead[:, 54:55, :] = own[:, EXTRA + 1 : EXTRA + 2, :]
-    ahead[:, 55:56, :] = own[:, EXTRA + 7 : EXTRA + 8, :]
-    above[...] = own[:, :48, :]
-
-
-def kernel(order_ref, order2_ref, own, ahead, above, below, out_ref):
+def halo_kernel(own, theirs, ahead, above, below, theirs_ref):
+    theirs_ref[...] = theirs[...]
+    for name, ref in (("ahead", ahead), ("above", above), ("below", below)):
+        taken = PARTS[name][0]
+        for k, rp in enumerate(taken):
+            start = TILES.index(rp) * 8
+            ref[:, k * 8 : k * 8 + 8, :] = own[:, start : start + 8, :]
+        if name != "ahead":
+            ref[:, len(taken) * 8 :, :] = own[:, ORB : ORB + 8, :]
+    last = [ORB + OWN.index(rp) for rp in AHEAD] + [EXTRA + 1, EXTRA + 1]
+    for k, row in enumerate(last):
+        ahead[:, 48 + k : 49 + k, :] = own[:, row : row + 1, :]
+
+
+def kernel(order_ref, order2_ref, theirs, own, ahead, above, below, out_ref):
     refs = {"own": own, "ahead": ahead, "above": above, "below": below}
     where = pieces()
     lane = lax.broadcasted_iota(jnp.int32, (8, 128), 1)
     trial_index, slab, freq = (lax.axis_index(a) for a in AXES)
-    block = (freq ^ (slab & 1)) * 16 + trial_index
+    block = (freq ^ (lax.div(slab + 1, 2) & 1)) * 16 + trial_index
 
     energy = own[:, EXTRA, :]
-    theirs = ahead[0, 55:56, :]
     a0 = a1 = a2 = a3 = jnp.zeros((16, 128), jnp.float32)
-    for scalars in (
-        [own[0, EXTRA + n : EXTRA + n + 1, :] for n in range(2, 7)],
-        [jnp.broadcast_to(theirs[:, n : n + 1], (1, 128)) for n in range(5)],
-    ):
-        k0, k1, k2, k3, shift = scalars
+    for ref, first in ((own.at[0], EXTRA + 2), (theirs, 2)):
+        k0, k1, k2, k3, shift = [ref[first + n : first + n + 1, :] for n in range(5)]
         c = (energy + shift) / 4.5
         b0, b1, b2, b3 = k0 - k2, k1 - 3.0 * k3, 2.0 * k2, 4.0 * k3
         a3 = a3 + b3
@@ -146,8 +153,6 @@
         if rp not in orb:
             name, _, row = where[rp]
             orb[rp] = refs[name][:, row, :]
-            if name == "ahead":
-                orb[rp] = orb[rp] * inside_plane(4)
         return orb[rp]
 
     def trial(rp):
@@ -278,15 +283,15 @@
 
 
 def device(block, slab):
-    return ((block % 16) * 8 + slab) * 2 + ((block // 16) ^ (slab & 1))
+    return ((block % 16) * 8 + slab) * 2 + half_of(slab, block // 16)
 
 
 def shift_perm(step, dslab):
     return [
-        (device(block + step, (slab + dslab) % 8), device(block, slab))
+        (device(block + step, slab + dslab), device(block, slab))
         for block in range(32)
         for slab in range(8)
-        if 0 <= block + step < 32
+        if 0 <= block + step < 32 and slab + dslab < 8
     ]
 
 
@@ -298,11 +303,11 @@
     def shape(rows, lead=(16,)):
         return jax.ShapeDtypeStruct((*lead, rows, 128), jnp.float32)
 
-    send = pl.pallas_call(
+    send, scalars = pl.pallas_call(
         pack_kernel,
-        out_shape=shape(len(TILES) * 8),
+        out_shape=[shape(len(TILES) * 8), shape(8, ())],
         in_specs=[smem] * 3 + [pl.BlockSpec(memory_space=pltpu.HBM)] * 3,
-        out_specs=vmem,
+        out_specs=[vmem] * 2,
         scratch_shapes=[
             pltpu.VMEM((1024, 128), jnp.float32),
             pltpu.VMEM((128, 128), jnp.float32),
@@ -313,24 +318,27 @@
     )(energies, cheb, shifts, trials.reshape(32, 64, 128), orbitals[0], potential)
     own = lax.all_to_all(send, "trial", split_axis=0, concat_axis=0, tiled=True)
 
-    ahead, above = pl.pallas_call(
+    theirs = lax.ppermute(scalars, "freq", [(0, 1), (1, 0)])
+
+    ahead, above, below, theirs = pl.pallas_call(
         halo_kernel,
-        out_shape=[shape(56), shape(48)],
-        in_specs=[vmem],
-        out_specs=[vmem] * 2,
+        out_shape=[shape(len(PARTS[name][0]) * 8 + 8) for name in ("ahead", "above", "below")]
+        + [shape(8, ())],
+        in_specs=[vmem] * 2,
+        out_specs=[vmem] * 4,
         compiler_params=params,
-    )(own)
+    )(own, theirs)
     ahead = lax.ppermute(ahead, AXES, shift_perm(0, 1))
-    below = lax.ppermute(own, AXES, shift_perm(-1, 0))
     above = lax.ppermute(above, AXES, shift_perm(1, 0))
+    below = lax.ppermute(below, AXES, shift_perm(-1, 0))
 
     partial = pl.pallas_call(
         kernel,
         out_shape=shape(256, ()),
-        in_specs=[vmem] * 6,
+        in_specs=[vmem] * 7,
         out_specs=vmem,
         compiler_params=params,
-    )(column_order[None], jnp.repeat(column_order, 2)[None], own, ahead, above, below)
+    )(column_order[None], jnp.repeat(column_order, 2)[None], theirs, own, ahead, above, below)
     terms = lax.all_to_all(partial, AXES, split_axis=0, concat_axis=0, tiled=True)
     return jnp.sum(terms, axis=0, keepdims=True)
 

time: 82 us -> 81 us (0.988)
  blocking collectives: 56.5 us -> 26.1 us
  waiting for transfers between devices: 6.45 us -> 24.1 us
  starting transfers between devices: 9.63 us -> 19.7 us
  local copies, waits for them, and re-layouts: 0.23 us -> 1.69 us
    all_to_all x1 -> x0, blocking collectives: 30.2 us -> none  [local(): own = lax.all_to_all(send, 'trial', split_axis=0, concat_axis=0, tiled=True)]
    all_to_all x0 -> x1, waiting for transfers between devices: none -> 15.9 us  [local(): own = lax.all_to_all(send, 'trial', split_axis=0, concat_axis=0, tiled=True)]
    all_to_all x0 -> x1, starting transfers between devices: none -> 9.99 us  [local(): own = lax.all_to_all(send, 'trial', split_axis=0, concat_axis=0, tiled=True)]
    ppermute x1, waiting for transfers between devices: 0.29 us -> 6.95 us  [local(): ahead = lax.ppermute(ahead, AXES, shift_perm(0, 1))]
    ppermute x1, waiting for transfers between devices: 6.15 us -> 0.01 us  [local(): above = lax.ppermute(above, AXES, shift_perm(1, 0))]
    ppermute x1 -> x2, starting transfers between devices: 1.93 us -> 6.5 us  [the longest x1 3.64 us: local(): below = lax.ppermute(below, AXES, shift_perm(-1, 0))]
    ppermute x1, starting transfers between devices: 5.01 us -> 1.29 us  [local(): ahead = lax.ppermute(ahead, AXES, shift_perm(0, 1))]
    ppermute x1 -> x2, waiting for transfers between devices: 0.01 us -> 1.22 us  [the longest x1 1.22 us: local(): theirs = lax.ppermute(scalars, 'freq', [(0, 1), (1, 0)])]
  transfers between devices with their start and end apart: 3 -> 5, of which waited for: 2 -> 3; matrix products, arithmetic and copies ran while one was open for 0% -> 2% of each run, Pallas kernels for 0% -> 0%
where the time goes in v3:
time: 81 us; the launch traced here: 80.6 us
  blocking collectives  26.1 us (32%)
  waiting for transfers between devices  24.1 us (30%)
  starting transfers between devices  19.7 us (24%)
  Pallas kernels  6.79 us (8%)
  local copies, waits for them, and re-layouts  1.69 us (2%)
  between operations  1.38 us (2%)
    all_to_all x1, blocking collectives, local(): lax.all_to_all(partial, AXES, split_axis=0, concat_axis=0, tiled=True)  26.1 us
    all_to_all x1, waiting for transfers between devices, local(): own = lax.all_to_all(send, 'trial', split_axis=0, concat_axis=0, tiled=True)  15.9 us
    all_to_all x1, starting transfers between devices, local(): own = lax.all_to_all(send, 'trial', split_axis=0, concat_axis=0, tiled=True)  9.99 us
    ppermute x1, waiting for transfers between devices, local(): ahead = lax.ppermute(ahead, AXES, shift_perm(0, 1))  6.95 us
    pallas_call x1, Pallas kernels, local(): pl.pallas_call(kernel, out_shape=shape(256, ()), in_specs=[vmem] * 7, out...  3.69 us
    ppermute x1, starting transfers between devices, local(): below = lax.ppermute(below, AXES, shift_perm(-1, 0))  3.64 us
    pallas_call x1, Pallas kernels, local(): pl.pallas_call(pack_kernel, out_shape=[shape(len(TILES) * 8), shape(8, ()...  2.97 us
    ppermute x1, starting transfers between devices, local(): theirs = lax.ppermute(scalars, 'freq', [(0, 1), (1, 0)])  2.85 us
  transfers between devices with their start and end apart: 5, of which 3 were waited for; matrix products, arithmetic and copies ran while one was open for 2% of the time, Pallas kernels for 0%

profile of v3, /device:TPU:1, one launch (start us, length us, event | category | flops | bytes accessed | tf_op | source)
XLA Modules:
  0.0 80.6 jit_solution(3134123049825881049)
XLA Ops:
  1.3 3.0 %shard_map.73 = (f32[16,80,128]{2,1,0:T(8,128)}, f32[8,128]{1,0:T(8,128)}) custom-call(f32[1]{0:T(128)S(6)} %copy.9.energy, f32[1,4]{1,0:T(1,128)} %cheb.1, f32[1]{0:T(128)S(6)} %copy.10.shift, f32[32,64,128]{2,1,0:T(8,128)} %bitcast.9, f32[4,64,128]{2,1,0:T(8,128)} %bitcast.10, f32[4,64,128]{2,1,0:T(8,128)} %potential_hbm.1), custom_call_target="tpu_custom_call" | custom-call | tf_op jit(solution)/shard_map/pallas_call | solution.py:306
  4.3 0.0 copy-start.1
  4.3 10.0 %all-to-all-start = ((f32[16,80,128]{2,1,0:T(8,128)}), f32[16,80,128]{2,1,0:T(8,128)S(1)}, u32[]{:S(2)}, u32[]{:S(2)}) async-start(f32[16,80,128]{2,1,0:T(8,128)} %get-tuple-element.11), calls=%async_computation | async-start | bytes 1310720 | tf_op jit(solution)/shard_map/all_to_all | solution.py:319
  14.3 0.0 copy-done.1
  14.3 2.9 %collective-permute-start = (f32[8,128]{1,0:T(8,128)S(1)}, f32[8,128]{1,0:T(8,128)S(1)}, u32[]{:S(2)}, u32[]{:S(2)}) collective-permute-start(f32[8,128]{1,0:T(8,128)S(1)} %copy-done.1), channel_id=1, source_target_pairs={{0,1},{1,0},{2,3},{3,2},{4,5},{5,4},{6,7},{7,6},{8,9},{9,8},{10,11... | collective-permute-start | bytes 12296 | tf_op jit(solution)/shard_map/ppermute | solution.py:321
  17.1 1.2 %collective-permute-done.theirs = f32[8,128]{1,0:T(8,128)S(1)} collective-permute-done((f32[8,128]{1,0:T(8,128)S(1)}, f32[8,128]{1,0:T(8,128)S(1)}, u32[]{:S(2)}, u32[]{:S(2)}) %collective-permute-start) | collective-permute-done | bytes 4128 | tf_op jit(solution)/shard_map/ppermute | solution.py:321
  18.4 15.9 %all-to-all-done.own = f32[16,80,128]{2,1,0:T(8,128)S(1)} async-done(((f32[16,80,128]{2,1,0:T(8,128)}), f32[16,80,128]{2,1,0:T(8,128)S(1)}, u32[]{:S(2)}, u32[]{:S(2)}) %all-to-all-start) | async-done | bytes 655392 | tf_op jit(solution)/shard_map/all_to_all | solution.py:319
  34.3 0.1 shard_map.74
  34.4 1.9 %collective-permute-start.2 = (f32[16,64,128]{2,1,0:T(8,128)S(1)}, f32[16,64,128]{2,1,0:T(8,128)S(1)}, u32[]{:S(2)}, u32[]{:S(2)}) collective-permute-start(f32[16,64,128]{2,1,0:T(8,128)S(1)} %get-tuple-element.15), channel_id=1, source_target_pairs={{16,0},{19,3},{21,5},{22,6},{24,8},{27,11},{29,13},{30,14},{32,16}... | collective-permute-start | bytes 1572872 | tf_op jit(solution)/shard_map/ppermute | solution.py:332
  36.4 0.0 copy-start
  36.4 1.3 %collective-permute-start.1 = (f32[16,56,128]{2,1,0:T(8,128)S(1)}, f32[16,56,128]{2,1,0:T(8,128)S(1)}, u32[]{:S(2)}, u32[]{:S(2)}) collective-permute-start(f32[16,56,128]{2,1,0:T(8,128)S(1)} %get-tuple-element.14), channel_id=1, source_target_pairs={{3,0},{5,3},{6,5},{8,6},{11,8},{13,11},{14,13},{19,16},{21,19},{22... | collective-permute-start | bytes 1376264 | tf_op jit(solution)/shard_map/ppermute | solution.py:331
  37.7 3.6 %collective-permute-start.3 = (f32[16,56,128]{2,1,0:T(8,128)S(1)}, f32[16,56,128]{2,1,0:T(8,128)S(1)}, u32[]{:S(2)}, u32[]{:S(2)}) collective-permute-start(f32[16,56,128]{2,1,0:T(8,128)S(1)} %get-tuple-element.16), channel_id=1, source_target_pairs={{0,16},{3,19},{5,21},{6,22},{8,24},{11,27},{13,29},{14,30},{16,32}... | collective-permute-start | bytes 1376264 | tf_op jit(solution)/shard_map/ppermute | solution.py:333
  41.3 0.0 copy-done
  41.3 0.7 broadcast_in_dim.10
  42.0 1.0 %broadcast_in_dim_reshape.3.order2_ref = s32[1,256]{1,0:T(1,128)S(1)} reshape(s32[128,2]{1,0:T(8,128)} %broadcast_in_dim.10) | data formatting | bytes 2048 | tf_op jit(solution)/shard_map/broadcast_in_dim;reshape | solution.py:341
  43.0 6.9 %collective-permute-done.1.ahead = f32[16,56,128]{2,1,0:T(8,128)S(1)} collective-permute-done((f32[16,56,128]{2,1,0:T(8,128)S(1)}, f32[16,56,128]{2,1,0:T(8,128)S(1)}, u32[]{:S(2)}, u32[]{:S(2)}) %collective-permute-start.1) | collective-permute-done | bytes 458784 | tf_op jit(solution)/shard_map/ppermute | solution.py:331
  50.0 0.0 collective-permute-done.3.below
  50.0 0.0 collective-permute-done.2.above
  50.0 3.7 %shard_map.75 = f32[256,128]{1,0:T(8,128)S(1)} custom-call(s32[1,128]{1,0:T(1,128)S(1)} %bitcast.8, s32[1,256]{1,0:T(1,128)S(1)} %broadcast_in_dim_reshape.3.order2_ref, f32[8,128]{1,0:T(8,128)S(1)} %get-tuple-element.13.theirs, f32[16,80,128]{2,1,0:T(8,128)S(1)} %all-to-all-done.own, f32[16,56,128]{2,1,0:T(8,128)S(1)} %collective-permute-done.1.ahead, ...), custom_call_target="tpu_custom_call" | custom-call | tf_op jit(solution)/shard_map/pallas_call | solution.py:335
  53.7 26.1 %all_to_all.14 = f32[256,1,128]{2,1,0:T(1,128)S(1)} all-to-all(f32[256,1,128]{2,1,0:T(1,128)S(1)} %bitcast.7), channel_id=1, replica_groups=mesh['trial'=16,'slab'=8,'freq'=2] {'trial','slab','freq'}, dimensions={0} | all-to-all | bytes 262144 | tf_op jit(solution)/shard_map/all_to_all | solution.py:342
  79.8 0.8 reduce_sum.9
Async XLA Ops:
  4.3 10.0 %copy-start.1 = (f32[8,128]{1,0:T(8,128)S(1)}, f32[8,128]{1,0:T(8,128)}, u32[]{:S(2)}) copy-start(f32[8,128]{1,0:T(8,128)} %get-tuple-element.12) | copy-start | bytes 12292
  4.3 30.0 %all-to-all-start = ((f32[16,80,128]{2,1,0:T(8,128)}), f32[16,80,128]{2,1,0:T(8,128)S(1)}, u32[]{:S(2)}, u32[]{:S(2)}) async-start(f32[16,80,128]{2,1,0:T(8,128)} %get-tuple-element.11), calls=%async_computation | async-start | bytes 1310720 | tf_op jit(solution)/shard_map/all_to_all | solution.py:319
  14.3 4.1 %collective-permute-start = (f32[8,128]{1,0:T(8,128)S(1)}, f32[8,128]{1,0:T(8,128)S(1)}, u32[]{:S(2)}, u32[]{:S(2)}) collective-permute-start(f32[8,128]{1,0:T(8,128)S(1)} %copy-done.1), channel_id=1, source_target_pairs={{0,1},{1,0},{2,3},{3,2},{4,5},{5,4},{6,7},{7,6},{8,9},{9,8},{10,11... | collective-permute-start | bytes 12296 | tf_op jit(solution)/shard_map/ppermute | solution.py:321
  34.4 15.5 %collective-permute-start.2 = (f32[16,64,128]{2,1,0:T(8,128)S(1)}, f32[16,64,128]{2,1,0:T(8,128)S(1)}, u32[]{:S(2)}, u32[]{:S(2)}) collective-permute-start(f32[16,64,128]{2,1,0:T(8,128)S(1)} %get-tuple-element.15), channel_id=1, source_target_pairs={{16,0},{19,3},{21,5},{22,6},{24,8},{27,11},{29,13},{30,14},{32,16}... | collective-permute-start | bytes 1572872 | tf_op jit(solution)/shard_map/ppermute | solution.py:332
  36.4 5.0 %copy-start = (s32[128]{0:T(128)S(1)}, s32[128]{0:T(128)}, u32[]{:S(2)}) copy-start(s32[128]{0:T(128)} %param.13) | copy-start | bytes 1540
  36.4 13.6 %collective-permute-start.1 = (f32[16,56,128]{2,1,0:T(8,128)S(1)}, f32[16,56,128]{2,1,0:T(8,128)S(1)}, u32[]{:S(2)}, u32[]{:S(2)}) collective-permute-start(f32[16,56,128]{2,1,0:T(8,128)S(1)} %get-tuple-element.14), channel_id=1, source_target_pairs={{3,0},{5,3},{6,5},{8,6},{11,8},{13,11},{14,13},{19,16},{21,19},{22... | collective-permute-start | bytes 1376264 | tf_op jit(solution)/shard_map/ppermute | solution.py:331
  37.7 12.3 %collective-permute-start.3 = (f32[16,56,128]{2,1,0:T(8,128)S(1)}, f32[16,56,128]{2,1,0:T(8,128)S(1)}, u32[]{:S(2)}, u32[]{:S(2)}) collective-permute-start(f32[16,56,128]{2,1,0:T(8,128)S(1)} %get-tuple-element.16), channel_id=1, source_target_pairs={{0,16},{3,19},{5,21},{6,22},{8,24},{11,27},{13,29},{14,30},{16,32}... | collective-permute-start | bytes 1376264 | tf_op jit(solution)/shard_map/ppermute | solution.py:333

commit v4 on v3

--- a/solution.py
+++ b/solution.py
@@ -1,3 +1,4 @@
+import functools
 import math
 
 import jax
@@ -9,7 +10,6 @@
 
 AXES = ("trial", "slab", "freq")
 HOP = 1.0 / 9.0
-HIGHEST = lax.Precision.HIGHEST
 
 TILES = [(0, 0), (0, 1), (0, 2), (0, 3), (1, 0), (1, 1), (1, 2), (1, 3), "o", "e"]
 ORB = TILES.index("o") * 8
@@ -128,8 +128,40 @@
         ahead[:, 48 + k : 49 + k, :] = own[:, row : row + 1, :]
 
 
-def kernel(order_ref, order2_ref, theirs, own, ahead, above, below, out_ref):
-    refs = {"own": own, "ahead": ahead, "above": above, "below": below}
+STAGES = (("own",), ("own", "ahead"), ("own", "ahead", "above", "below"))
+
+
+def stage_of(where, a, b, dz):
+    names = {where[a][0], where[b][0]}
+    if a == b and dz == 0 and a[1] == 3:
+        names.add("ahead")
+    return next(n for n, held in enumerate(STAGES) if names <= set(held))
+
+
+def halves(x):
+    high = x.astype(jnp.bfloat16)
+    return high, (x - high.astype(jnp.float32)).astype(jnp.bfloat16)
+
+
+def thirds(x):
+    high = x.astype(jnp.bfloat16)
+    middle, low = halves(x - high.astype(jnp.float32))
+    return high, middle, low
+
+
+def product(lefts, rights, left_dim, right_dim):
+    return lax.dot_general(
+        jnp.concatenate(lefts, axis=left_dim), jnp.concatenate(rights, axis=right_dim),
+        (((left_dim,), (right_dim,)), ((), ())), preferred_element_type=jnp.float32,
+    )
+
+
+def kernel(stage, *args):
+    count = 2 if stage == 0 else 1
+    out_ref, *pick_ref = args[-count:]
+    args = args[:-count]
+    refs = dict(zip(STAGES[stage], args[-len(STAGES[stage]) :]))
+    own, ahead, theirs = refs["own"], refs.get("ahead"), args[0]
     where = pieces()
     lane = lax.broadcasted_iota(jnp.int32, (8, 128), 1)
     trial_index, slab, freq = (lax.axis_index(a) for a in AXES)
@@ -237,8 +269,8 @@
         for m, h in enumerate(powers(a, b, dz)):
             if h is None:
                 continue
-            product = left[m] * right
-            term = (product[:8] + product[8:]) * h
+            both = left[m] * right
+            term = (both[:8] + both[8:]) * h
             total = term if total is None else total + term
         for s in (4, 2, 1):
             total = total + pltpu.roll(total, s, 0)
@@ -248,14 +280,22 @@
             total = total * inside_z(-dz)
         return total
 
-    gram = jnp.zeros((128, 128), jnp.float32)
+    if stage == 0:
+        gram = jnp.zeros((128, 128), jnp.float32)
+        rows = lax.broadcasted_iota(jnp.int32, (128, 128), 0)
+        pick_ref[0][...] = (args[1][...] == rows).astype(jnp.float32)
+    else:
+        gram = args[1][...]
+    lefts, sides = [], []
     for a, rights in pairs().items():
         response = None
         for dz in range(-3, 4):
             todo = []
             for b in rights:
                 dist = abs(a[0] - b[0]) + abs(a[1] - b[1]) + abs(dz)
-                if dist <= 3 and (a != b or dz == 0 or (dz > 0 and a[1] < 4)):
+                if dist > 3 or stage_of(where, a, b, dz) != stage:
+                    continue
+                if a != b or dz == 0 or (dz > 0 and a[1] < 4):
                     todo.append((b, dist))
             if not todo:
                 continue
@@ -268,18 +308,27 @@
                 acc = term if acc is None else acc + term
             acc = turn(acc.reshape(128, 128), -dz)
             response = acc if response is None else response + acc
-        gram = gram + lax.dot_general(
-            trial(a).reshape(128, 128), response, (((1,), (1,)), ((), ())),
-            precision=HIGHEST, preferred_element_type=jnp.float32,
-        )
-
+        if response is None:
+            continue
+        high, low = halves(trial(a).reshape(128, 128))
+        other, rest = halves(response)
+        lefts += [high, high, low]
+        sides += [other, rest, other]
+        if len(lefts) == 6:
+            gram = gram + product(lefts, sides, 1, 1)
+            lefts, sides = [], []
+    if lefts:
+        gram = gram + product(lefts, sides, 1, 1)
+
+    if stage < 2:
+        out_ref[...] = gram
+        return
     gram = (gram + gram.T) * (1.0 / math.sqrt(32 * 64 * 128 * 16))
-    pick = (order_ref[...] == lax.broadcasted_iota(jnp.int32, (128, 128), 0)).astype(jnp.float32)
-    pick2 = (order2_ref[...] == lax.broadcasted_iota(jnp.int32, (128, 256), 0)).astype(jnp.float32)
-    gram = jnp.dot(gram, pick, precision=HIGHEST, preferred_element_type=jnp.float32)
-    out_ref[...] = lax.dot_general(
-        pick2, gram, (((0,), (0,)), ((), ())), precision=HIGHEST, preferred_element_type=jnp.float32
-    )
+    pick = args[2][...].astype(jnp.bfloat16)
+    gram = product(thirds(gram), [pick] * 3, 1, 0)
+    gram = product([pick] * 3, thirds(gram), 0, 0)
+    for n in range(2):
+        out_ref[pl.ds(n, 128, stride=2), :] = gram
 
 
 def device(block, slab):
@@ -332,13 +381,25 @@
     above = lax.ppermute(above, AXES, shift_perm(1, 0))
     below = lax.ppermute(below, AXES, shift_perm(-1, 0))
 
-    partial = pl.pallas_call(
-        kernel,
-        out_shape=shape(256, ()),
-        in_specs=[vmem] * 7,
-        out_specs=vmem,
-        compiler_params=params,
-    )(column_order[None], jnp.repeat(column_order, 2)[None], theirs, own, ahead, above, below)
+    arrays = {"own": own, "ahead": ahead, "above": above, "below": below}
+    partial = pick = None
+    for stage, names in enumerate(STAGES):
+        operands = [theirs, column_order[None] if stage == 0 else partial]
+        if stage == 2:
+            operands.append(pick)
+        operands += [arrays[name] for name in names]
+        shapes = [shape(256 if stage == 2 else 128, ())]
+        if stage == 0:
+            shapes.append(shape(128, ()))
+        partial, *rest = pl.pallas_call(
+            functools.partial(kernel, stage),
+            out_shape=shapes,
+            in_specs=[vmem] * len(operands),
+            out_specs=[vmem] * len(shapes),
+            compiler_params=params,
+            cost_estimate=pl.CostEstimate(flops=2 * 10**9, bytes_accessed=3 * 2**20, transcendentals=0),
+        )(*operands)
+        pick = rest[0] if rest else pick
     terms = lax.all_to_all(partial, AXES, split_axis=0, concat_axis=0, tiled=True)
     return jnp.sum(terms, axis=0, keepdims=True)
 

time: 81 us -> 76.9 us (0.949)
  waiting for transfers between devices: 24.1 us -> 21.6 us
  blocking collectives: 26.1 us -> 24.7 us
  local copies, waits for them, and re-layouts: 1.69 us -> 0.65 us
  Pallas kernels: 6.79 us -> 7.66 us
    ppermute x1, waiting for transfers between devices: 6.95 us -> 4.48 us  [local(): ahead = lax.ppermute(ahead, AXES, shift_perm(0, 1))]
    all_to_all x1, blocking collectives: 26.1 us -> 24.7 us  [local(): lax.all_to_all(partial, AXES, split_axis=0, concat_axis=0, tiled=True)]
    another operation x1 -> x0, local copies, waits for them, and re-layouts: 0.97 us -> none  [local(): jnp.repeat(column_order, 2)[None]]
    pallas_call x1 -> x3, Pallas kernels: 3.69 us -> 4.56 us  [local(): pl.pallas_call(functools.partial(kernel, stage), out_shape=shapes, in_spe...]
  transfers between devices with their start and end apart: 5 -> 5, of which waited for: 3 -> 3; matrix products, arithmetic and copies ran while one was open for 2% -> 0% of each run, Pallas kernels for 0% -> 4%
where the time goes in v4:
time: 76.9 us; the launch traced here: 76.6 us
  blocking collectives  24.7 us (32%)
  waiting for transfers between devices  21.6 us (28%)
  starting transfers between devices  19.7 us (26%)
  Pallas kernels  7.66 us (10%)
  between operations  1.4 us (2%)
  other arithmetic  0.79 us (1%)
    all_to_all x1, blocking collectives, local(): lax.all_to_all(partial, AXES, split_axis=0, concat_axis=0, tiled=True)  24.7 us
    all_to_all x1, waiting for transfers between devices, local(): own = lax.all_to_all(send, 'trial', split_axis=0, concat_axis=0, tiled=True)  15.9 us
    all_to_all x1, starting transfers between devices, local(): own = lax.all_to_all(send, 'trial', split_axis=0, concat_axis=0, tiled=True)  9.99 us
    pallas_call x3, Pallas kernels, local(): pl.pallas_call(functools.partial(kernel, stage), out_shape=shapes, in_spe...  4.56 us
    ppermute x1, waiting for transfers between devices, local(): ahead = lax.ppermute(ahead, AXES, shift_perm(0, 1))  4.48 us
    ppermute x1, starting transfers between devices, local(): below = lax.ppermute(below, AXES, shift_perm(-1, 0))  3.64 us
    pallas_call x1, Pallas kernels, local(): pl.pallas_call(pack_kernel, out_shape=[shape(len(TILES) * 8), shape(8, ()...  2.97 us
    ppermute x1, starting transfers between devices, local(): theirs = lax.ppermute(scalars, 'freq', [(0, 1), (1, 0)])  2.85 us
  transfers between devices with their start and end apart: 5, of which 3 were waited for; matrix products, arithmetic and copies ran while one was open for 0% of the time, Pallas kernels for 4%

profile of v4, /device:TPU:1, one launch (start us, length us, event | category | flops | bytes accessed | tf_op | source)
XLA Modules:
  0.0 76.6 jit_solution(12254479750129744538)
XLA Ops:
  1.3 3.0 %shard_map.73 = (f32[16,80,128]{2,1,0:T(8,128)}, f32[8,128]{1,0:T(8,128)}) custom-call(f32[1]{0:T(128)S(6)} %copy.9.energy, f32[1,4]{1,0:T(1,128)} %cheb.1, f32[1]{0:T(128)S(6)} %copy.10.shift, f32[32,64,128]{2,1,0:T(8,128)} %bitcast.9, f32[4,64,128]{2,1,0:T(8,128)} %bitcast.10, f32[4,64,128]{2,1,0:T(8,128)} %potential_hbm.1), custom_call_target="tpu_custom_call" | custom-call | tf_op jit(solution)/shard_map/pallas_call | solution.py:355
  4.3 0.0 copy-start.1
  4.3 10.0 %all-to-all-start = ((f32[16,80,128]{2,1,0:T(8,128)}), f32[16,80,128]{2,1,0:T(8,128)S(1)}, u32[]{:S(2)}, u32[]{:S(2)}) async-start(f32[16,80,128]{2,1,0:T(8,128)} %get-tuple-element.13), calls=%async_computation | async-start | bytes 1310720 | tf_op jit(solution)/shard_map/all_to_all | solution.py:368
  14.3 0.0 copy-done.1
  14.3 2.9 %collective-permute-start = (f32[8,128]{1,0:T(8,128)S(1)}, f32[8,128]{1,0:T(8,128)S(1)}, u32[]{:S(2)}, u32[]{:S(2)}) collective-permute-start(f32[8,128]{1,0:T(8,128)S(1)} %copy-done.1), channel_id=1, source_target_pairs={{0,1},{1,0},{2,3},{3,2},{4,5},{5,4},{6,7},{7,6},{8,9},{9,8},{10,11... | collective-permute-start | bytes 12296 | tf_op jit(solution)/shard_map/ppermute | solution.py:370
  17.1 1.2 %collective-permute-done.theirs = f32[8,128]{1,0:T(8,128)S(1)} collective-permute-done((f32[8,128]{1,0:T(8,128)S(1)}, f32[8,128]{1,0:T(8,128)S(1)}, u32[]{:S(2)}, u32[]{:S(2)}) %collective-permute-start) | collective-permute-done | bytes 4128 | tf_op jit(solution)/shard_map/ppermute | solution.py:370
  18.4 15.9 %all-to-all-done.own.args_2_.args_3_ = f32[16,80,128]{2,1,0:T(8,128)S(1)} async-done(((f32[16,80,128]{2,1,0:T(8,128)}), f32[16,80,128]{2,1,0:T(8,128)S(1)}, u32[]{:S(2)}, u32[]{:S(2)}) %all-to-all-start) | async-done | bytes 655392 | tf_op jit(solution)/shard_map/all_to_all | solution.py:368
  34.3 0.1 shard_map.74
  34.4 1.3 %collective-permute-start.1 = (f32[16,56,128]{2,1,0:T(8,128)S(1)}, f32[16,56,128]{2,1,0:T(8,128)S(1)}, u32[]{:S(2)}, u32[]{:S(2)}) collective-permute-start(f32[16,56,128]{2,1,0:T(8,128)S(1)} %get-tuple-element.17), channel_id=1, source_target_pairs={{3,0},{5,3},{6,5},{8,6},{11,8},{13,11},{14,13},{19,16},{21,19},{22... | collective-permute-start | bytes 1376264 | tf_op jit(solution)/shard_map/ppermute | solution.py:380
  35.7 1.9 %collective-permute-start.2 = (f32[16,64,128]{2,1,0:T(8,128)S(1)}, f32[16,64,128]{2,1,0:T(8,128)S(1)}, u32[]{:S(2)}, u32[]{:S(2)}) collective-permute-start(f32[16,64,128]{2,1,0:T(8,128)S(1)} %get-tuple-element.19), channel_id=1, source_target_pairs={{16,0},{19,3},{21,5},{22,6},{24,8},{27,11},{29,13},{30,14},{32,16}... | collective-permute-start | bytes 1572872 | tf_op jit(solution)/shard_map/ppermute | solution.py:381
  37.7 3.6 %collective-permute-start.3 = (f32[16,56,128]{2,1,0:T(8,128)S(1)}, f32[16,56,128]{2,1,0:T(8,128)S(1)}, u32[]{:S(2)}, u32[]{:S(2)}) collective-permute-start(f32[16,56,128]{2,1,0:T(8,128)S(1)} %get-tuple-element.20), channel_id=1, source_target_pairs={{0,16},{3,19},{5,21},{6,22},{8,24},{11,27},{13,29},{14,30},{16,32}... | collective-permute-start | bytes 1376264 | tf_op jit(solution)/shard_map/ppermute | solution.py:382
  41.3 0.0 copy-start
  41.3 0.6 copy-done
  42.0 2.2 %shard_map.75 = (f32[128,128]{1,0:T(8,128)S(1)}, f32[128,128]{1,0:T(8,128)S(1)}) custom-call(f32[8,128]{1,0:T(8,128)S(1)} %get-tuple-element.15.args_0_, s32[1,128]{1,0:T(1,128)S(1)} %bitcast.8, f32[16,80,128]{2,1,0:T(8,128)S(1)} %all-to-all-done.own.args_2_.args_3_), custom_call_target="tpu_custom_call" | custom-call | flops 2000000000 | bytes 3145728 | tf_op jit(solution)/shard_map/pallas_call | solution.py:394
  44.2 4.5 %collective-permute-done.1.args_3_.args_4_ = f32[16,56,128]{2,1,0:T(8,128)S(1)} collective-permute-done((f32[16,56,128]{2,1,0:T(8,128)S(1)}, f32[16,56,128]{2,1,0:T(8,128)S(1)}, u32[]{:S(2)}, u32[]{:S(2)}) %collective-permute-start.1) | collective-permute-done | bytes 458784 | tf_op jit(solution)/shard_map/ppermute | solution.py:380
  48.7 0.7 shard_map.76.args_1_
  49.4 0.0 collective-permute-done.3.args_6_
  49.4 0.0 collective-permute-done.2.args_5_
  49.4 1.7 %shard_map.77 = f32[256,128]{1,0:T(8,128)S(1)} custom-call(f32[8,128]{1,0:T(8,128)S(1)} %get-tuple-element.15.args_0_, f32[128,128]{1,0:T(8,128)S(1)} %shard_map.76.args_1_, f32[128,128]{1,0:T(8,128)S(1)} %get-tuple-element.18.args_2_, f32[16,80,128]{2,1,0:T(8,128)S(1)} %all-to-all-done.own.args_2_.args_3_, ...), custom_call_target="tpu_custom_call" | custom-call | flops 2000000000 | bytes 3145728 | tf_op jit(solution)/shard_map/pallas_call | solution.py:394
  51.1 24.7 %all_to_all.14 = f32[256,1,128]{2,1,0:T(1,128)S(1)} all-to-all(f32[256,1,128]{2,1,0:T(1,128)S(1)} %bitcast.7), channel_id=1, replica_groups=mesh['trial'=16,'slab'=8,'freq'=2] {'trial','slab','freq'}, dimensions={0} | all-to-all | bytes 262144 | tf_op jit(solution)/shard_map/all_to_all | solution.py:403
  75.8 0.8 %reduce_sum.9 = f32[128]{0:T(128)} reduce(f32[256,1,128]{2,1,0:T(1,128)S(1)} %all_to_all.14, f32[]{:T(128)} %constant.0.clone.1), dimensions={0,1}, to_apply=%region_0.0 | reduce | flops 32640 | bytes 131588 | tf_op jit(solution)/shard_map/reduce_sum | solution.py:404
Async XLA Ops:
  4.3 10.0 %copy-start.1 = (f32[8,128]{1,0:T(8,128)S(1)}, f32[8,128]{1,0:T(8,128)}, u32[]{:S(2)}) copy-start(f32[8,128]{1,0:T(8,128)} %get-tuple-element.14) | copy-start | bytes 12292
  4.3 30.0 %all-to-all-start = ((f32[16,80,128]{2,1,0:T(8,128)}), f32[16,80,128]{2,1,0:T(8,128)S(1)}, u32[]{:S(2)}, u32[]{:S(2)}) async-start(f32[16,80,128]{2,1,0:T(8,128)} %get-tuple-element.13), calls=%async_computation | async-start | bytes 1310720 | tf_op jit(solution)/shard_map/all_to_all | solution.py:368
  14.3 4.1 %collective-permute-start = (f32[8,128]{1,0:T(8,128)S(1)}, f32[8,128]{1,0:T(8,128)S(1)}, u32[]{:S(2)}, u32[]{:S(2)}) collective-permute-start(f32[8,128]{1,0:T(8,128)S(1)} %copy-done.1), channel_id=1, source_target_pairs={{0,1},{1,0},{2,3},{3,2},{4,5},{5,4},{6,7},{7,6},{8,9},{9,8},{10,11... | collective-permute-start | bytes 12296 | tf_op jit(solution)/shard_map/ppermute | solution.py:370
  34.4 14.2 %collective-permute-start.1 = (f32[16,56,128]{2,1,0:T(8,128)S(1)}, f32[16,56,128]{2,1,0:T(8,128)S(1)}, u32[]{:S(2)}, u32[]{:S(2)}) collective-permute-start(f32[16,56,128]{2,1,0:T(8,128)S(1)} %get-tuple-element.17), channel_id=1, source_target_pairs={{3,0},{5,3},{6,5},{8,6},{11,8},{13,11},{14,13},{19,16},{21,19},{22... | collective-permute-start | bytes 1376264 | tf_op jit(solution)/shard_map/ppermute | solution.py:380
  35.7 13.6 %collective-permute-start.2 = (f32[16,64,128]{2,1,0:T(8,128)S(1)}, f32[16,64,128]{2,1,0:T(8,128)S(1)}, u32[]{:S(2)}, u32[]{:S(2)}) collective-permute-start(f32[16,64,128]{2,1,0:T(8,128)S(1)} %get-tuple-element.19), channel_id=1, source_target_pairs={{16,0},{19,3},{21,5},{22,6},{24,8},{27,11},{29,13},{30,14},{32,16}... | collective-permute-start | bytes 1572872 | tf_op jit(solution)/shard_map/ppermute | solution.py:381
  37.7 11.7 %collective-permute-start.3 = (f32[16,56,128]{2,1,0:T(8,128)S(1)}, f32[16,56,128]{2,1,0:T(8,128)S(1)}, u32[]{:S(2)}, u32[]{:S(2)}) collective-permute-start(f32[16,56,128]{2,1,0:T(8,128)S(1)} %get-tuple-element.20), channel_id=1, source_target_pairs={{0,16},{3,19},{5,21},{6,22},{8,24},{11,27},{13,29},{14,30},{16,32}... | collective-permute-start | bytes 1376264 | tf_op jit(solution)/shard_map/ppermute | solution.py:382
  41.3 0.7 copy-start

commit v5 on v4

--- a/solution.py
+++ b/solution.py
@@ -14,6 +14,7 @@
 TILES = [(0, 0), (0, 1), (0, 2), (0, 3), (1, 0), (1, 1), (1, 2), (1, 3), "o", "e"]
 ORB = TILES.index("o") * 8
 EXTRA = TILES.index("e") * 8
+SENT = EXTRA + 2
 OWN = [(row, plane) for row in range(2) for plane in range(4)]
 PARTS = {
     "ahead": ([(row, plane) for row in range(2) for plane in range(3)], 0, 4),
@@ -102,20 +103,30 @@
     for copy in copies:
         copy.wait()
     for t in range(16):
+        base = t * SENT
         for k, tile in enumerate(TILES):
             if tile == "o":
                 for row in range(2):
-                    out_ref[t, k * 8 + 4 * row : k * 8 + 4 * row + 4, :] = orbital[pl.ds(2 * t + row, 4, stride=32), :]
+                    out_ref[base + k * 8 + 4 * row : base + k * 8 + 4 * row + 4, :] = orbital[
+                        pl.ds(2 * t + row, 4, stride=32), :
+                    ]
             elif tile == "e":
                 y = jnp.clip(half * 32 + 2 * t + lax.rem(trial, 4) - 1, 0, 63)
                 at = potential[pl.ds(lax.div(trial, 4) * 64 + y, 1), :]
-                out_ref[t, k * 8 : k * 8 + 8, :] = jnp.where(row_of == 1, at, scalars)
+                out_ref[base + k * 8 : base + k * 8 + 2, :] = jnp.where(row_of == 1, at, scalars)[:2]
             else:
-                out_ref[t, k * 8 : k * 8 + 8, :] = trials[pl.ds(tile[1] * 32 + 2 * t + tile[0], 8, stride=128), :]
-
-
-def halo_kernel(own, theirs, ahead, above, below, theirs_ref):
+                out_ref[base + k * 8 : base + k * 8 + 8, :] = trials[
+                    pl.ds(tile[1] * 32 + 2 * t + tile[0], 8, stride=128), :
+                ]
+
+
+def halo_kernel(raw, ours, theirs, ahead, above, below, theirs_ref, own):
     theirs_ref[...] = theirs[...]
+    for s in range(16):
+        for first in range(0, SENT, 8):
+            size = min(8, SENT - first)
+            own[s, first : first + size, :] = raw[s * SENT + first : s * SENT + first + size, :]
+        own[s, SENT:, :] = ours[2:, :]
     for name, ref in (("ahead", ahead), ("above", above), ("below", below)):
         taken = PARTS[name][0]
         for k, rp in enumerate(taken):
@@ -354,7 +365,7 @@
 
     send, scalars = pl.pallas_call(
         pack_kernel,
-        out_shape=[shape(len(TILES) * 8), shape(8, ())],
+        out_shape=[shape(16 * SENT, ()), shape(8, ())],
         in_specs=[smem] * 3 + [pl.BlockSpec(memory_space=pltpu.HBM)] * 3,
         out_specs=[vmem] * 2,
         scratch_shapes=[
@@ -365,18 +376,18 @@
         ],
         compiler_params=pltpu.CompilerParams(vmem_limit_bytes=60 * 1024 * 1024),
     )(energies, cheb, shifts, trials.reshape(32, 64, 128), orbitals[0], potential)
-    own = lax.all_to_all(send, "trial", split_axis=0, concat_axis=0, tiled=True)
+    raw = lax.all_to_all(send.reshape(16 * SENT, 1, 128), "trial", split_axis=0, concat_axis=0, tiled=True)
 
     theirs = lax.ppermute(scalars, "freq", [(0, 1), (1, 0)])
 
-    ahead, above, below, theirs = pl.pallas_call(
+    ahead, above, below, theirs, own = pl.pallas_call(
         halo_kernel,
         out_shape=[shape(len(PARTS[name][0]) * 8 + 8) for name in ("ahead", "above", "below")]
-        + [shape(8, ())],
-        in_specs=[vmem] * 2,
-        out_specs=[vmem] * 4,
+        + [shape(8, ()), shape(len(TILES) * 8)],
+        in_specs=[vmem] * 3,
+        out_specs=[vmem] * 5,
         compiler_params=params,
-    )(own, theirs)
+    )(raw.reshape(16 * SENT, 128), scalars, theirs)
     ahead = lax.ppermute(ahead, AXES, shift_perm(0, 1))
     above = lax.ppermute(above, AXES, shift_perm(1, 0))
     below = lax.ppermute(below, AXES, shift_perm(-1, 0))

time: 76.9 us -> 76.1 us (0.990)
  waiting for transfers between devices: 21.6 us -> 20.8 us
    all_to_all x1, waiting for transfers between devices: 15.9 us -> 14.9 us  [local(): lax.all_to_all(send.reshape(16 * SENT, 1, 128), 'trial', split_axis=0, co...]
where the time goes in v5:
time: 76.1 us; the launch traced here: 75.8 us
  blocking collectives  24.7 us (32%)
  waiting for transfers between devices  20.8 us (27%)
  starting transfers between devices  19.7 us (26%)
  Pallas kernels  7.69 us (10%)
  between operations  1.4 us (2%)
  other arithmetic  0.79 us (1%)
    all_to_all x1, blocking collectives, local(): lax.all_to_all(partial, AXES, split_axis=0, concat_axis=0, tiled=True)  24.7 us
    all_to_all x1, waiting for transfers between devices, local(): lax.all_to_all(send.reshape(16 * SENT, 1, 128), 'trial', split_axis=0, co...  14.9 us
    all_to_all x1, starting transfers between devices, local(): lax.all_to_all(send.reshape(16 * SENT, 1, 128), 'trial', split_axis=0, co...  9.99 us
    ppermute x1, waiting for transfers between devices, local(): ahead = lax.ppermute(ahead, AXES, shift_perm(0, 1))  4.65 us
    pallas_call x3, Pallas kernels, local(): pl.pallas_call(functools.partial(kernel, stage), out_shape=shapes, in_spe...  4.57 us
    ppermute x1, starting transfers between devices, local(): below = lax.ppermute(below, AXES, shift_perm(-1, 0))  3.64 us
    pallas_call x1, Pallas kernels, local(): pl.pallas_call(pack_kernel, out_shape=[shape(16 * SENT, ()), shape(8, ())...  2.95 us
    ppermute x1, starting transfers between devices, local(): theirs = lax.ppermute(scalars, 'freq', [(0, 1), (1, 0)])  2.85 us
  transfers between devices with their start and end apart: 5, of which 3 were waited for; matrix products, arithmetic and copies ran while one was open for 0% of the time, Pallas kernels for 4%

profile of v5, /device:TPU:1, one launch (start us, length us, event | category | flops | bytes accessed | tf_op | source)
XLA Modules:
  0.0 75.8 jit_solution(2312908512626146366)
XLA Ops:
  1.3 3.0 %shard_map.73 = (f32[1184,128]{1,0:T(8,128)}, f32[8,128]{1,0:T(8,128)}) custom-call(f32[1]{0:T(128)S(6)} %copy.10.energy, f32[1,4]{1,0:T(1,128)} %cheb.1, f32[1]{0:T(128)S(6)} %copy.11.shift, f32[32,64,128]{2,1,0:T(8,128)} %bitcast.14, f32[4,64,128]{2,1,0:T(8,128)} %bitcast.16, f32[4,64,128]{2,1,0:T(8,128)} %potential_hbm.1), custom_call_target="tpu_custom_call" | custom-call | tf_op jit(solution)/shard_map/pallas_call | solution.py:366
  4.3 0.0 copy-start
  4.3 10.0 %all-to-all-start = ((f32[1184,1,128]{2,1,0:T(1,128)}), f32[1184,1,128]{2,1,0:T(1,128)S(1)}, u32[]{:S(2)}, u32[]{:S(2)}) async-start(f32[1184,1,128]{2,1,0:T(1,128)} %bitcast.15), calls=%async_computation | async-start | bytes 1212416 | tf_op jit(solution)/shard_map/all_to_all | solution.py:379
  14.3 0.0 copy-done
  14.3 2.9 %collective-permute-start = (f32[8,128]{1,0:T(8,128)S(1)}, f32[8,128]{1,0:T(8,128)S(1)}, u32[]{:S(2)}, u32[]{:S(2)}) collective-permute-start(f32[8,128]{1,0:T(8,128)S(1)} %copy-done), channel_id=1, source_target_pairs={{0,1},{1,0},{2,3},{3,2},{4,5},{5,4},{6,7},{7,6},{8,9},{9,8},{10,11... | collective-permute-start | bytes 12296 | tf_op jit(solution)/shard_map/ppermute | solution.py:381
  17.1 1.2 %collective-permute-done.theirs = f32[8,128]{1,0:T(8,128)S(1)} collective-permute-done((f32[8,128]{1,0:T(8,128)S(1)}, f32[8,128]{1,0:T(8,128)S(1)}, u32[]{:S(2)}, u32[]{:S(2)}) %collective-permute-start) | collective-permute-done | bytes 4128 | tf_op jit(solution)/shard_map/ppermute | solution.py:381
  18.3 14.9 %all-to-all-done = f32[1184,1,128]{2,1,0:T(1,128)S(1)} async-done(((f32[1184,1,128]{2,1,0:T(1,128)}), f32[1184,1,128]{2,1,0:T(1,128)S(1)}, u32[]{:S(2)}, u32[]{:S(2)}) %all-to-all-start) | async-done | bytes 606240 | tf_op jit(solution)/shard_map/all_to_all | solution.py:379
  33.3 0.2 shard_map.74
  33.5 1.3 %collective-permute-start.1 = (f32[16,56,128]{2,1,0:T(8,128)S(1)}, f32[16,56,128]{2,1,0:T(8,128)S(1)}, u32[]{:S(2)}, u32[]{:S(2)}) collective-permute-start(f32[16,56,128]{2,1,0:T(8,128)S(1)} %get-tuple-element.19), channel_id=1, source_target_pairs={{3,0},{5,3},{6,5},{8,6},{11,8},{13,11},{14,13},{19,16},{21,19},{22... | collective-permute-start | bytes 1376264 | tf_op jit(solution)/shard_map/ppermute | solution.py:391
  34.8 1.9 %collective-permute-start.2 = (f32[16,64,128]{2,1,0:T(8,128)S(1)}, f32[16,64,128]{2,1,0:T(8,128)S(1)}, u32[]{:S(2)}, u32[]{:S(2)}) collective-permute-start(f32[16,64,128]{2,1,0:T(8,128)S(1)} %get-tuple-element.21), channel_id=1, source_target_pairs={{16,0},{19,3},{21,5},{22,6},{24,8},{27,11},{29,13},{30,14},{32,16}... | collective-permute-start | bytes 1572872 | tf_op jit(solution)/shard_map/ppermute | solution.py:392
  36.7 3.6 %collective-permute-start.3 = (f32[16,56,128]{2,1,0:T(8,128)S(1)}, f32[16,56,128]{2,1,0:T(8,128)S(1)}, u32[]{:S(2)}, u32[]{:S(2)}) collective-permute-start(f32[16,56,128]{2,1,0:T(8,128)S(1)} %get-tuple-element.22), channel_id=1, source_target_pairs={{0,16},{3,19},{5,21},{6,22},{8,24},{11,27},{13,29},{14,30},{16,32}... | collective-permute-start | bytes 1376264 | tf_op jit(solution)/shard_map/ppermute | solution.py:393
  40.3 0.0 copy-start.1
  40.3 0.6 copy-done.1
  41.0 2.2 %shard_map.75 = (f32[128,128]{1,0:T(8,128)S(1)}, f32[128,128]{1,0:T(8,128)S(1)}) custom-call(f32[8,128]{1,0:T(8,128)S(1)} %get-tuple-element.16.args_0_, s32[1,128]{1,0:T(1,128)S(1)} %bitcast.13, f32[16,80,128]{2,1,0:T(8,128)S(1)} %get-tuple-element.17.args_2_.args_3_), custom_call_target="tpu_custom_call" | custom-call | flops 2000000000 | bytes 3145728 | tf_op jit(solution)/shard_map/pallas_call | solution.py:405
  43.2 4.7 %collective-permute-done.1.args_3_.args_4_ = f32[16,56,128]{2,1,0:T(8,128)S(1)} collective-permute-done((f32[16,56,128]{2,1,0:T(8,128)S(1)}, f32[16,56,128]{2,1,0:T(8,128)S(1)}, u32[]{:S(2)}, u32[]{:S(2)}) %collective-permute-start.1) | collective-permute-done | bytes 458784 | tf_op jit(solution)/shard_map/ppermute | solution.py:391
  47.8 0.7 shard_map.76.args_1_
  48.6 0.0 collective-permute-done.3.args_6_
  48.6 0.0 collective-permute-done.2.args_5_
  48.6 1.7 %shard_map.77 = f32[256,128]{1,0:T(8,128)S(1)} custom-call(f32[8,128]{1,0:T(8,128)S(1)} %get-tuple-element.16.args_0_, f32[128,128]{1,0:T(8,128)S(1)} %shard_map.76.args_1_, f32[128,128]{1,0:T(8,128)S(1)} %get-tuple-element.20.args_2_, f32[16,80,128]{2,1,0:T(8,128)S(1)} %get-tuple-element.17.args_2_.args_3_, ...), custom_call_target="tpu_custom_call" | custom-call | flops 2000000000 | bytes 3145728 | tf_op jit(solution)/shard_map/pallas_call | solution.py:405
  50.3 24.7 %all_to_all.14 = f32[256,1,128]{2,1,0:T(1,128)S(1)} all-to-all(f32[256,1,128]{2,1,0:T(1,128)S(1)} %bitcast.12), channel_id=1, replica_groups=mesh['trial'=16,'slab'=8,'freq'=2] {'trial','slab','freq'}, dimensions={0} | all-to-all | bytes 262144 | tf_op jit(solution)/shard_map/all_to_all | solution.py:414
  75.0 0.8 %reduce_sum.9 = f32[128]{0:T(128)} reduce(f32[256,1,128]{2,1,0:T(1,128)S(1)} %all_to_all.14, f32[]{:T(128)} %constant.0.clone.1), dimensions={0,1}, to_apply=%region_0.0 | reduce | flops 32640 | bytes 131588 | tf_op jit(solution)/shard_map/reduce_sum | solution.py:415
Async XLA Ops:
  4.3 10.0 %copy-start = (f32[8,128]{1,0:T(8,128)S(1)}, f32[8,128]{1,0:T(8,128)}, u32[]{:S(2)}) copy-start(f32[8,128]{1,0:T(8,128)} %get-tuple-element.15.ours) | copy-start | bytes 12292
  4.3 29.0 %all-to-all-start = ((f32[1184,1,128]{2,1,0:T(1,128)}), f32[1184,1,128]{2,1,0:T(1,128)S(1)}, u32[]{:S(2)}, u32[]{:S(2)}) async-start(f32[1184,1,128]{2,1,0:T(1,128)} %bitcast.15), calls=%async_computation | async-start | bytes 1212416 | tf_op jit(solution)/shard_map/all_to_all | solution.py:379
  14.3 4.1 %collective-permute-start = (f32[8,128]{1,0:T(8,128)S(1)}, f32[8,128]{1,0:T(8,128)S(1)}, u32[]{:S(2)}, u32[]{:S(2)}) collective-permute-start(f32[8,128]{1,0:T(8,128)S(1)} %copy-done), channel_id=1, source_target_pairs={{0,1},{1,0},{2,3},{3,2},{4,5},{5,4},{6,7},{7,6},{8,9},{9,8},{10,11... | collective-permute-start | bytes 12296 | tf_op jit(solution)/shard_map/ppermute | solution.py:381
  33.5 14.4 %collective-permute-start.1 = (f32[16,56,128]{2,1,0:T(8,128)S(1)}, f32[16,56,128]{2,1,0:T(8,128)S(1)}, u32[]{:S(2)}, u32[]{:S(2)}) collective-permute-start(f32[16,56,128]{2,1,0:T(8,128)S(1)} %get-tuple-element.19), channel_id=1, source_target_pairs={{3,0},{5,3},{6,5},{8,6},{11,8},{13,11},{14,13},{19,16},{21,19},{22... | collective-permute-start | bytes 1376264 | tf_op jit(solution)/shard_map/ppermute | solution.py:391
  34.8 13.8 %collective-permute-start.2 = (f32[16,64,128]{2,1,0:T(8,128)S(1)}, f32[16,64,128]{2,1,0:T(8,128)S(1)}, u32[]{:S(2)}, u32[]{:S(2)}) collective-permute-start(f32[16,64,128]{2,1,0:T(8,128)S(1)} %get-tuple-element.21), channel_id=1, source_target_pairs={{16,0},{19,3},{21,5},{22,6},{24,8},{27,11},{29,13},{30,14},{32,16}... | collective-permute-start | bytes 1572872 | tf_op jit(solution)/shard_map/ppermute | solution.py:392
  36.7 11.9 %collective-permute-start.3 = (f32[16,56,128]{2,1,0:T(8,128)S(1)}, f32[16,56,128]{2,1,0:T(8,128)S(1)}, u32[]{:S(2)}, u32[]{:S(2)}) collective-permute-start(f32[16,56,128]{2,1,0:T(8,128)S(1)} %get-tuple-element.22), channel_id=1, source_target_pairs={{0,16},{3,19},{5,21},{6,22},{8,24},{11,27},{13,29},{14,30},{16,32}... | collective-permute-start | bytes 1376264 | tf_op jit(solution)/shard_map/ppermute | solution.py:393
  40.3 0.7 copy-start.1

commit v6 on v5

--- a/solution.py
+++ b/solution.py
@@ -27,11 +27,11 @@
 def pieces():
     table = {}
     for rp in OWN:
-        table[rp] = ("own", TILES.index(rp) * 8, ORB + OWN.index(rp))
+        table[rp] = ("own", TILES.index(rp) * 8, ORB, OWN.index(rp))
     for name, (taken, drow, dplane) in PARTS.items():
         for k, rp in enumerate(taken):
             orb = k if name == "ahead" else OWN.index(rp)
-            table[(rp[0] + drow, rp[1] + dplane)] = (name, k * 8, len(taken) * 8 + orb)
+            table[(rp[0] + drow, rp[1] + dplane)] = (name, k * 8, len(taken) * 8, orb)
     return table
 
 
@@ -127,6 +127,10 @@
             size = min(8, SENT - first)
             own[s, first : first + size, :] = raw[s * SENT + first : s * SENT + first + size, :]
         own[s, SENT:, :] = ours[2:, :]
+    for k in range(8):
+        orbs = raw[pl.ds(ORB + k, 16, stride=SENT), :]
+        own[2 * k, ORB : ORB + 8, :] = orbs[:8]
+        own[2 * k + 1, ORB : ORB + 8, :] = orbs[8:]
     for name, ref in (("ahead", ahead), ("above", above), ("below", below)):
         taken = PARTS[name][0]
         for k, rp in enumerate(taken):
@@ -134,9 +138,13 @@
             ref[:, k * 8 : k * 8 + 8, :] = own[:, start : start + 8, :]
         if name != "ahead":
             ref[:, len(taken) * 8 :, :] = own[:, ORB : ORB + 8, :]
-    last = [ORB + OWN.index(rp) for rp in AHEAD] + [EXTRA + 1, EXTRA + 1]
-    for k, row in enumerate(last):
-        ahead[:, 48 + k : 49 + k, :] = own[:, row : row + 1, :]
+    for k, rp in enumerate(AHEAD):
+        start = 2 * OWN.index(rp)
+        ahead[2 * k : 2 * k + 2, 48:, :] = own[start : start + 2, ORB : ORB + 8, :]
+    levels = raw[pl.ds(EXTRA + 1, 16, stride=SENT), :]
+    for k in (12, 14):
+        ahead[k, 48:, :] = levels[:8]
+        ahead[k + 1, 48:, :] = levels[8:]
 
 
 STAGES = (("own",), ("own", "ahead"), ("own", "ahead", "above", "below"))
@@ -194,12 +202,12 @@
 
     def orbital(rp):
         if rp not in orb:
-            name, _, row = where[rp]
-            orb[rp] = refs[name][:, row, :]
+            name, _, row, k = where[rp]
+            orb[rp] = jnp.concatenate([refs[name][2 * k + n, row : row + 8, :] for n in range(2)], axis=0)
         return orb[rp]
 
     def trial(rp):
-        name, row, _ = where[rp]
+        name, row, _, _ = where[rp]
         return refs[name][:, row : row + 8, :]
 
     def turn(x, dz):
@@ -220,9 +228,12 @@
 
     def potential(row, plane):
         if (row, plane) not in pot:
-            ref, at = (own, EXTRA + 1) if plane < 4 else (ahead, 54)
             source = plane % 4 * 4 + row + 1
-            pot[(row, plane)] = jnp.broadcast_to(ref[source, at : at + 1, :] / 4.5, (8, 128))
+            if plane < 4:
+                at = own[source, EXTRA + 1 : EXTRA + 2, :]
+            else:
+                at = ahead[12 + source // 8, 48 + source % 8 : 49 + source % 8, :]
+            pot[(row, plane)] = jnp.broadcast_to(at / 4.5, (8, 128))
         return pot[(row, plane)]
 
     ones = jnp.ones((8, 128), jnp.float32)

time: 76.1 us -> 76 us (level)
  no operation moved by 1% of the time
where the time goes in v6:
time: 76 us; the launch traced here: 75.7 us
  blocking collectives  24.7 us (32%)
  waiting for transfers between devices  20.8 us (27%)
  starting transfers between devices  19.7 us (26%)
  Pallas kernels  7.58 us (10%)
  between operations  1.4 us (2%)
  other arithmetic  0.79 us (1%)
    all_to_all x1, blocking collectives, local(): lax.all_to_all(partial, AXES, split_axis=0, concat_axis=0, tiled=True)  24.7 us
    all_to_all x1, waiting for transfers between devices, local(): lax.all_to_all(send.reshape(16 * SENT, 1, 128), 'trial', split_axis=0, co...  14.9 us
    all_to_all x1, starting transfers between devices, local(): lax.all_to_all(send.reshape(16 * SENT, 1, 128), 'trial', split_axis=0, co...  9.99 us
    ppermute x1, waiting for transfers between devices, local(): ahead = lax.ppermute(ahead, AXES, shift_perm(0, 1))  4.68 us
    pallas_call x3, Pallas kernels, local(): pl.pallas_call(functools.partial(kernel, stage), out_shape=shapes, in_spe...  4.48 us
    ppermute x1, starting transfers between devices, local(): below = lax.ppermute(below, AXES, shift_perm(-1, 0))  3.64 us
    pallas_call x1, Pallas kernels, local(): pl.pallas_call(pack_kernel, out_shape=[shape(16 * SENT, ()), shape(8, ())...  2.95 us
    ppermute x1, starting transfers between devices, local(): theirs = lax.ppermute(scalars, 'freq', [(0, 1), (1, 0)])  2.85 us
  transfers between devices with their start and end apart: 5, of which 3 were waited for; matrix products, arithmetic and copies ran while one was open for 0% of the time, Pallas kernels for 4%

profile of v6, /device:TPU:1, one launch (start us, length us, event | category | flops | bytes accessed | tf_op | source)
XLA Modules:
  0.0 75.7 jit_solution(9412599542829646602)
XLA Ops:
  1.3 3.0 %shard_map.73 = (f32[1184,128]{1,0:T(8,128)}, f32[8,128]{1,0:T(8,128)}) custom-call(f32[1]{0:T(128)S(6)} %copy.10.energy, f32[1,4]{1,0:T(1,128)} %cheb.1, f32[1]{0:T(128)S(6)} %copy.11.shift, f32[32,64,128]{2,1,0:T(8,128)} %bitcast.14, f32[4,64,128]{2,1,0:T(8,128)} %bitcast.16, f32[4,64,128]{2,1,0:T(8,128)} %potential_hbm.1), custom_call_target="tpu_custom_call" | custom-call | tf_op jit(solution)/shard_map/pallas_call | solution.py:377
  4.3 0.0 copy-start
  4.3 10.0 %all-to-all-start = ((f32[1184,1,128]{2,1,0:T(1,128)}), f32[1184,1,128]{2,1,0:T(1,128)S(1)}, u32[]{:S(2)}, u32[]{:S(2)}) async-start(f32[1184,1,128]{2,1,0:T(1,128)} %bitcast.15), calls=%async_computation | async-start | bytes 1212416 | tf_op jit(solution)/shard_map/all_to_all | solution.py:390
  14.3 0.0 copy-done
  14.3 2.9 %collective-permute-start = (f32[8,128]{1,0:T(8,128)S(1)}, f32[8,128]{1,0:T(8,128)S(1)}, u32[]{:S(2)}, u32[]{:S(2)}) collective-permute-start(f32[8,128]{1,0:T(8,128)S(1)} %copy-done), channel_id=1, source_target_pairs={{0,1},{1,0},{2,3},{3,2},{4,5},{5,4},{6,7},{7,6},{8,9},{9,8},{10,11... | collective-permute-start | bytes 12296 | tf_op jit(solution)/shard_map/ppermute | solution.py:392
  17.1 1.2 %collective-permute-done.theirs = f32[8,128]{1,0:T(8,128)S(1)} collective-permute-done((f32[8,128]{1,0:T(8,128)S(1)}, f32[8,128]{1,0:T(8,128)S(1)}, u32[]{:S(2)}, u32[]{:S(2)}) %collective-permute-start) | collective-permute-done | bytes 4128 | tf_op jit(solution)/shard_map/ppermute | solution.py:392
  18.3 14.9 %all-to-all-done = f32[1184,1,128]{2,1,0:T(1,128)S(1)} async-done(((f32[1184,1,128]{2,1,0:T(1,128)}), f32[1184,1,128]{2,1,0:T(1,128)S(1)}, u32[]{:S(2)}, u32[]{:S(2)}) %all-to-all-start) | async-done | bytes 606240 | tf_op jit(solution)/shard_map/all_to_all | solution.py:390
  33.3 0.1 shard_map.74
  33.4 1.3 %collective-permute-start.1 = (f32[16,56,128]{2,1,0:T(8,128)S(1)}, f32[16,56,128]{2,1,0:T(8,128)S(1)}, u32[]{:S(2)}, u32[]{:S(2)}) collective-permute-start(f32[16,56,128]{2,1,0:T(8,128)S(1)} %get-tuple-element.19), channel_id=1, source_target_pairs={{3,0},{5,3},{6,5},{8,6},{11,8},{13,11},{14,13},{19,16},{21,19},{22... | collective-permute-start | bytes 1376264 | tf_op jit(solution)/shard_map/ppermute | solution.py:402
  34.7 1.9 %collective-permute-start.2 = (f32[16,64,128]{2,1,0:T(8,128)S(1)}, f32[16,64,128]{2,1,0:T(8,128)S(1)}, u32[]{:S(2)}, u32[]{:S(2)}) collective-permute-start(f32[16,64,128]{2,1,0:T(8,128)S(1)} %get-tuple-element.21), channel_id=1, source_target_pairs={{16,0},{19,3},{21,5},{22,6},{24,8},{27,11},{29,13},{30,14},{32,16}... | collective-permute-start | bytes 1572872 | tf_op jit(solution)/shard_map/ppermute | solution.py:403
  36.7 3.6 %collective-permute-start.3 = (f32[16,56,128]{2,1,0:T(8,128)S(1)}, f32[16,56,128]{2,1,0:T(8,128)S(1)}, u32[]{:S(2)}, u32[]{:S(2)}) collective-permute-start(f32[16,56,128]{2,1,0:T(8,128)S(1)} %get-tuple-element.22), channel_id=1, source_target_pairs={{0,16},{3,19},{5,21},{6,22},{8,24},{11,27},{13,29},{14,30},{16,32}... | collective-permute-start | bytes 1376264 | tf_op jit(solution)/shard_map/ppermute | solution.py:404
  40.3 0.0 copy-start.1
  40.3 0.6 copy-done.1
  41.0 2.2 %shard_map.75 = (f32[128,128]{1,0:T(8,128)S(1)}, f32[128,128]{1,0:T(8,128)S(1)}) custom-call(f32[8,128]{1,0:T(8,128)S(1)} %get-tuple-element.16.args_0_, s32[1,128]{1,0:T(1,128)S(1)} %bitcast.13, f32[16,80,128]{2,1,0:T(8,128)S(1)} %get-tuple-element.17.args_2_.args_3_), custom_call_target="tpu_custom_call" | custom-call | flops 2000000000 | bytes 3145728 | tf_op jit(solution)/shard_map/pallas_call | solution.py:416
  43.1 4.7 %collective-permute-done.1.args_3_.args_4_ = f32[16,56,128]{2,1,0:T(8,128)S(1)} collective-permute-done((f32[16,56,128]{2,1,0:T(8,128)S(1)}, f32[16,56,128]{2,1,0:T(8,128)S(1)}, u32[]{:S(2)}, u32[]{:S(2)}) %collective-permute-start.1) | collective-permute-done | bytes 458784 | tf_op jit(solution)/shard_map/ppermute | solution.py:402
  47.8 0.7 shard_map.76.args_1_
  48.5 0.0 collective-permute-done.3.args_6_
  48.5 0.0 collective-permute-done.2.args_5_
  48.5 1.6 %shard_map.77 = f32[256,128]{1,0:T(8,128)S(1)} custom-call(f32[8,128]{1,0:T(8,128)S(1)} %get-tuple-element.16.args_0_, f32[128,128]{1,0:T(8,128)S(1)} %shard_map.76.args_1_, f32[128,128]{1,0:T(8,128)S(1)} %get-tuple-element.20.args_2_, f32[16,80,128]{2,1,0:T(8,128)S(1)} %get-tuple-element.17.args_2_.args_3_, ...), custom_call_target="tpu_custom_call" | custom-call | flops 2000000000 | bytes 3145728 | tf_op jit(solution)/shard_map/pallas_call | solution.py:416
  50.2 24.7 %all_to_all.14 = f32[256,1,128]{2,1,0:T(1,128)S(1)} all-to-all(f32[256,1,128]{2,1,0:T(1,128)S(1)} %bitcast.12), channel_id=1, replica_groups=mesh['trial'=16,'slab'=8,'freq'=2] {'trial','slab','freq'}, dimensions={0} | all-to-all | bytes 262144 | tf_op jit(solution)/shard_map/all_to_all | solution.py:425
  74.9 0.8 %reduce_sum.9 = f32[128]{0:T(128)} reduce(f32[256,1,128]{2,1,0:T(1,128)S(1)} %all_to_all.14, f32[]{:T(128)} %constant.0.clone.1), dimensions={0,1}, to_apply=%region_0.0 | reduce | flops 32640 | bytes 131588 | tf_op jit(solution)/shard_map/reduce_sum | solution.py:426
Async XLA Ops:
  4.3 10.0 %copy-start = (f32[8,128]{1,0:T(8,128)S(1)}, f32[8,128]{1,0:T(8,128)}, u32[]{:S(2)}) copy-start(f32[8,128]{1,0:T(8,128)} %get-tuple-element.15.ours) | copy-start | bytes 12292
  4.3 29.0 %all-to-all-start = ((f32[1184,1,128]{2,1,0:T(1,128)}), f32[1184,1,128]{2,1,0:T(1,128)S(1)}, u32[]{:S(2)}, u32[]{:S(2)}) async-start(f32[1184,1,128]{2,1,0:T(1,128)} %bitcast.15), calls=%async_computation | async-start | bytes 1212416 | tf_op jit(solution)/shard_map/all_to_all | solution.py:390
  14.3 4.1 %collective-permute-start = (f32[8,128]{1,0:T(8,128)S(1)}, f32[8,128]{1,0:T(8,128)S(1)}, u32[]{:S(2)}, u32[]{:S(2)}) collective-permute-start(f32[8,128]{1,0:T(8,128)S(1)} %copy-done), channel_id=1, source_target_pairs={{0,1},{1,0},{2,3},{3,2},{4,5},{5,4},{6,7},{7,6},{8,9},{9,8},{10,11... | collective-permute-start | bytes 12296 | tf_op jit(solution)/shard_map/ppermute | solution.py:392
  33.4 14.4 %collective-permute-start.1 = (f32[16,56,128]{2,1,0:T(8,128)S(1)}, f32[16,56,128]{2,1,0:T(8,128)S(1)}, u32[]{:S(2)}, u32[]{:S(2)}) collective-permute-start(f32[16,56,128]{2,1,0:T(8,128)S(1)} %get-tuple-element.19), channel_id=1, source_target_pairs={{3,0},{5,3},{6,5},{8,6},{11,8},{13,11},{14,13},{19,16},{21,19},{22... | collective-permute-start | bytes 1376264 | tf_op jit(solution)/shard_map/ppermute | solution.py:402
  34.7 13.8 %collective-permute-start.2 = (f32[16,64,128]{2,1,0:T(8,128)S(1)}, f32[16,64,128]{2,1,0:T(8,128)S(1)}, u32[]{:S(2)}, u32[]{:S(2)}) collective-permute-start(f32[16,64,128]{2,1,0:T(8,128)S(1)} %get-tuple-element.21), channel_id=1, source_target_pairs={{16,0},{19,3},{21,5},{22,6},{24,8},{27,11},{29,13},{30,14},{32,16}... | collective-permute-start | bytes 1572872 | tf_op jit(solution)/shard_map/ppermute | solution.py:403
  36.7 11.8 %collective-permute-start.3 = (f32[16,56,128]{2,1,0:T(8,128)S(1)}, f32[16,56,128]{2,1,0:T(8,128)S(1)}, u32[]{:S(2)}, u32[]{:S(2)}) collective-permute-start(f32[16,56,128]{2,1,0:T(8,128)S(1)} %get-tuple-element.22), channel_id=1, source_target_pairs={{0,16},{3,19},{5,21},{6,22},{8,24},{11,27},{13,29},{14,30},{16,32}... | collective-permute-start | bytes 1376264 | tf_op jit(solution)/shard_map/ppermute | solution.py:404
  40.3 0.7 copy-start.1

commit v7 on v5

--- a/solution.py
+++ b/solution.py
@@ -152,12 +152,6 @@
 def halves(x):
     high = x.astype(jnp.bfloat16)
     return high, (x - high.astype(jnp.float32)).astype(jnp.bfloat16)
-
-
-def thirds(x):
-    high = x.astype(jnp.bfloat16)
-    middle, low = halves(x - high.astype(jnp.float32))
-    return high, middle, low
 
 
 def product(lefts, rights, left_dim, right_dim):
@@ -336,8 +330,8 @@
         return
     gram = (gram + gram.T) * (1.0 / math.sqrt(32 * 64 * 128 * 16))
     pick = args[2][...].astype(jnp.bfloat16)
-    gram = product(thirds(gram), [pick] * 3, 1, 0)
-    gram = product([pick] * 3, thirds(gram), 0, 0)
+    gram = product(halves(gram), [pick] * 2, 1, 0)
+    gram = product([pick] * 2, halves(gram), 0, 0)
     for n in range(2):
         out_ref[pl.ds(n, 128, stride=2), :] = gram
 

time: 76.1 us -> 76.1 us (level)
  no operation moved by 1% of the time
where the time goes in v7:
time: 76.1 us; the launch traced here: 75.7 us
  blocking collectives  24.7 us (32%)
  waiting for transfers between devices  20.8 us (27%)
  starting transfers between devices  19.7 us (26%)
  Pallas kernels  7.65 us (10%)
  between operations  1.4 us (2%)
  other arithmetic  0.79 us (1%)
    all_to_all x1, blocking collectives, local(): lax.all_to_all(partial, AXES, split_axis=0, concat_axis=0, tiled=True)  24.7 us
    all_to_all x1, waiting for transfers between devices, local(): lax.all_to_all(send.reshape(16 * SENT, 1, 128), 'trial', split_axis=0, co...  14.9 us
    all_to_all x1, starting transfers between devices, local(): lax.all_to_all(send.reshape(16 * SENT, 1, 128), 'trial', split_axis=0, co...  9.99 us
    ppermute x1, waiting for transfers between devices, local(): ahead = lax.ppermute(ahead, AXES, shift_perm(0, 1))  4.65 us
    pallas_call x3, Pallas kernels, local(): pl.pallas_call(functools.partial(kernel, stage), out_shape=shapes, in_spe...  4.53 us
    ppermute x1, starting transfers between devices, local(): below = lax.ppermute(below, AXES, shift_perm(-1, 0))  3.64 us
    pallas_call x1, Pallas kernels, local(): pl.pallas_call(pack_kernel, out_shape=[shape(16 * SENT, ()), shape(8, ())...  2.95 us
    ppermute x1, starting transfers between devices, local(): theirs = lax.ppermute(scalars, 'freq', [(0, 1), (1, 0)])  2.85 us
  transfers between devices with their start and end apart: 5, of which 3 were waited for; matrix products, arithmetic and copies ran while one was open for 0% of the time, Pallas kernels for 4%

profile of v7, /device:TPU:1, one launch (start us, length us, event | category | flops | bytes accessed | tf_op | source)
XLA Modules:
  0.0 75.7 jit_solution(15277203630845930535)
XLA Ops:
  1.3 3.0 %shard_map.73 = (f32[1184,128]{1,0:T(8,128)}, f32[8,128]{1,0:T(8,128)}) custom-call(f32[1]{0:T(128)S(6)} %copy.10.energy, f32[1,4]{1,0:T(1,128)} %cheb.1, f32[1]{0:T(128)S(6)} %copy.11.shift, f32[32,64,128]{2,1,0:T(8,128)} %bitcast.14, f32[4,64,128]{2,1,0:T(8,128)} %bitcast.16, f32[4,64,128]{2,1,0:T(8,128)} %potential_hbm.1), custom_call_target="tpu_custom_call" | custom-call | tf_op jit(solution)/shard_map/pallas_call | solution.py:360
  4.3 0.0 copy-start
  4.3 10.0 %all-to-all-start = ((f32[1184,1,128]{2,1,0:T(1,128)}), f32[1184,1,128]{2,1,0:T(1,128)S(1)}, u32[]{:S(2)}, u32[]{:S(2)}) async-start(f32[1184,1,128]{2,1,0:T(1,128)} %bitcast.15), calls=%async_computation | async-start | bytes 1212416 | tf_op jit(solution)/shard_map/all_to_all | solution.py:373
  14.3 0.0 copy-done
  14.3 2.9 %collective-permute-start = (f32[8,128]{1,0:T(8,128)S(1)}, f32[8,128]{1,0:T(8,128)S(1)}, u32[]{:S(2)}, u32[]{:S(2)}) collective-permute-start(f32[8,128]{1,0:T(8,128)S(1)} %copy-done), channel_id=1, source_target_pairs={{0,1},{1,0},{2,3},{3,2},{4,5},{5,4},{6,7},{7,6},{8,9},{9,8},{10,11... | collective-permute-start | bytes 12296 | tf_op jit(solution)/shard_map/ppermute | solution.py:375
  17.1 1.2 %collective-permute-done.theirs = f32[8,128]{1,0:T(8,128)S(1)} collective-permute-done((f32[8,128]{1,0:T(8,128)S(1)}, f32[8,128]{1,0:T(8,128)S(1)}, u32[]{:S(2)}, u32[]{:S(2)}) %collective-permute-start) | collective-permute-done | bytes 4128 | tf_op jit(solution)/shard_map/ppermute | solution.py:375
  18.3 14.9 %all-to-all-done = f32[1184,1,128]{2,1,0:T(1,128)S(1)} async-done(((f32[1184,1,128]{2,1,0:T(1,128)}), f32[1184,1,128]{2,1,0:T(1,128)S(1)}, u32[]{:S(2)}, u32[]{:S(2)}) %all-to-all-start) | async-done | bytes 606240 | tf_op jit(solution)/shard_map/all_to_all | solution.py:373
  33.3 0.2 shard_map.74
  33.5 1.3 %collective-permute-start.1 = (f32[16,56,128]{2,1,0:T(8,128)S(1)}, f32[16,56,128]{2,1,0:T(8,128)S(1)}, u32[]{:S(2)}, u32[]{:S(2)}) collective-permute-start(f32[16,56,128]{2,1,0:T(8,128)S(1)} %get-tuple-element.19), channel_id=1, source_target_pairs={{3,0},{5,3},{6,5},{8,6},{11,8},{13,11},{14,13},{19,16},{21,19},{22... | collective-permute-start | bytes 1376264 | tf_op jit(solution)/shard_map/ppermute | solution.py:385
  34.8 1.9 %collective-permute-start.2 = (f32[16,64,128]{2,1,0:T(8,128)S(1)}, f32[16,64,128]{2,1,0:T(8,128)S(1)}, u32[]{:S(2)}, u32[]{:S(2)}) collective-permute-start(f32[16,64,128]{2,1,0:T(8,128)S(1)} %get-tuple-element.21), channel_id=1, source_target_pairs={{16,0},{19,3},{21,5},{22,6},{24,8},{27,11},{29,13},{30,14},{32,16}... | collective-permute-start | bytes 1572872 | tf_op jit(solution)/shard_map/ppermute | solution.py:386
  36.7 3.6 %collective-permute-start.3 = (f32[16,56,128]{2,1,0:T(8,128)S(1)}, f32[16,56,128]{2,1,0:T(8,128)S(1)}, u32[]{:S(2)}, u32[]{:S(2)}) collective-permute-start(f32[16,56,128]{2,1,0:T(8,128)S(1)} %get-tuple-element.22), channel_id=1, source_target_pairs={{0,16},{3,19},{5,21},{6,22},{8,24},{11,27},{13,29},{14,30},{16,32}... | collective-permute-start | bytes 1376264 | tf_op jit(solution)/shard_map/ppermute | solution.py:387
  40.3 0.0 copy-start.1
  40.3 0.6 copy-done.1
  41.0 2.2 %shard_map.75 = (f32[128,128]{1,0:T(8,128)S(1)}, f32[128,128]{1,0:T(8,128)S(1)}) custom-call(f32[8,128]{1,0:T(8,128)S(1)} %get-tuple-element.16.args_0_, s32[1,128]{1,0:T(1,128)S(1)} %bitcast.13, f32[16,80,128]{2,1,0:T(8,128)S(1)} %get-tuple-element.17.args_2_.args_3_), custom_call_target="tpu_custom_call" | custom-call | flops 2000000000 | bytes 3145728 | tf_op jit(solution)/shard_map/pallas_call | solution.py:399
  43.2 4.7 %collective-permute-done.1.args_3_.args_4_ = f32[16,56,128]{2,1,0:T(8,128)S(1)} collective-permute-done((f32[16,56,128]{2,1,0:T(8,128)S(1)}, f32[16,56,128]{2,1,0:T(8,128)S(1)}, u32[]{:S(2)}, u32[]{:S(2)}) %collective-permute-start.1) | collective-permute-done | bytes 458784 | tf_op jit(solution)/shard_map/ppermute | solution.py:385
  47.8 0.7 shard_map.76.args_1_
  48.6 0.0 collective-permute-done.3.args_6_
  48.6 0.0 collective-permute-done.2.args_5_
  48.6 1.6 %shard_map.77 = f32[256,128]{1,0:T(8,128)S(1)} custom-call(f32[8,128]{1,0:T(8,128)S(1)} %get-tuple-element.16.args_0_, f32[128,128]{1,0:T(8,128)S(1)} %shard_map.76.args_1_, f32[128,128]{1,0:T(8,128)S(1)} %get-tuple-element.20.args_2_, f32[16,80,128]{2,1,0:T(8,128)S(1)} %get-tuple-element.17.args_2_.args_3_, ...), custom_call_target="tpu_custom_call" | custom-call | flops 2000000000 | bytes 3145728 | tf_op jit(solution)/shard_map/pallas_call | solution.py:399
  50.2 24.7 %all_to_all.14 = f32[256,1,128]{2,1,0:T(1,128)S(1)} all-to-all(f32[256,1,128]{2,1,0:T(1,128)S(1)} %bitcast.12), channel_id=1, replica_groups=mesh['trial'=16,'slab'=8,'freq'=2] {'trial','slab','freq'}, dimensions={0} | all-to-all | bytes 262144 | tf_op jit(solution)/shard_map/all_to_all | solution.py:408
  74.9 0.8 %reduce_sum.9 = f32[128]{0:T(128)} reduce(f32[256,1,128]{2,1,0:T(1,128)S(1)} %all_to_all.14, f32[]{:T(128)} %constant.0.clone.1), dimensions={0,1}, to_apply=%region_0.0 | reduce | flops 32640 | bytes 131588 | tf_op jit(solution)/shard_map/reduce_sum | solution.py:409
Async XLA Ops:
  4.3 10.0 %copy-start = (f32[8,128]{1,0:T(8,128)S(1)}, f32[8,128]{1,0:T(8,128)}, u32[]{:S(2)}) copy-start(f32[8,128]{1,0:T(8,128)} %get-tuple-element.15.ours) | copy-start | bytes 12292
  4.3 29.0 %all-to-all-start = ((f32[1184,1,128]{2,1,0:T(1,128)}), f32[1184,1,128]{2,1,0:T(1,128)S(1)}, u32[]{:S(2)}, u32[]{:S(2)}) async-start(f32[1184,1,128]{2,1,0:T(1,128)} %bitcast.15), calls=%async_computation | async-start | bytes 1212416 | tf_op jit(solution)/shard_map/all_to_all | solution.py:373
  14.3 4.1 %collective-permute-start = (f32[8,128]{1,0:T(8,128)S(1)}, f32[8,128]{1,0:T(8,128)S(1)}, u32[]{:S(2)}, u32[]{:S(2)}) collective-permute-start(f32[8,128]{1,0:T(8,128)S(1)} %copy-done), channel_id=1, source_target_pairs={{0,1},{1,0},{2,3},{3,2},{4,5},{5,4},{6,7},{7,6},{8,9},{9,8},{10,11... | collective-permute-start | bytes 12296 | tf_op jit(solution)/shard_map/ppermute | solution.py:375
  33.5 14.4 %collective-permute-start.1 = (f32[16,56,128]{2,1,0:T(8,128)S(1)}, f32[16,56,128]{2,1,0:T(8,128)S(1)}, u32[]{:S(2)}, u32[]{:S(2)}) collective-permute-start(f32[16,56,128]{2,1,0:T(8,128)S(1)} %get-tuple-element.19), channel_id=1, source_target_pairs={{3,0},{5,3},{6,5},{8,6},{11,8},{13,11},{14,13},{19,16},{21,19},{22... | collective-permute-start | bytes 1376264 | tf_op jit(solution)/shard_map/ppermute | solution.py:385
  34.8 13.8 %collective-permute-start.2 = (f32[16,64,128]{2,1,0:T(8,128)S(1)}, f32[16,64,128]{2,1,0:T(8,128)S(1)}, u32[]{:S(2)}, u32[]{:S(2)}) collective-permute-start(f32[16,64,128]{2,1,0:T(8,128)S(1)} %get-tuple-element.21), channel_id=1, source_target_pairs={{16,0},{19,3},{21,5},{22,6},{24,8},{27,11},{29,13},{30,14},{32,16}... | collective-permute-start | bytes 1572872 | tf_op jit(solution)/shard_map/ppermute | solution.py:386
  36.7 11.9 %collective-permute-start.3 = (f32[16,56,128]{2,1,0:T(8,128)S(1)}, f32[16,56,128]{2,1,0:T(8,128)S(1)}, u32[]{:S(2)}, u32[]{:S(2)}) collective-permute-start(f32[16,56,128]{2,1,0:T(8,128)S(1)} %get-tuple-element.22), channel_id=1, source_target_pairs={{0,16},{3,19},{5,21},{6,22},{8,24},{11,27},{13,29},{14,30},{16,32}... | collective-permute-start | bytes 1376264 | tf_op jit(solution)/shard_map/ppermute | solution.py:387
  40.3 0.7 copy-start.1

commit v8 on v5

--- a/solution.py
+++ b/solution.py
@@ -18,8 +18,8 @@
 OWN = [(row, plane) for row in range(2) for plane in range(4)]
 PARTS = {
     "ahead": ([(row, plane) for row in range(2) for plane in range(3)], 0, 4),
-    "above": ([(0, 0), (0, 1), (0, 2), (0, 3), (1, 0), (1, 1), (1, 3)], 2, 0),
-    "below": ([(1, 0), (1, 1), (1, 2), (1, 3), (0, 2), (0, 3)], -2, 0),
+    "above": ([(0, 0), (0, 1), (0, 2), (0, 3), (1, 1), (1, 3)], 2, 0),
+    "below": ([(1, 0), (1, 1), (1, 2), (1, 3), (0, 0), (0, 2), (0, 3)], -2, 0),
 }
 AHEAD = PARTS["ahead"][0]
 
@@ -57,10 +57,10 @@
         if a[0] == 1:
             for plane in range(4):
                 add(a, (-1, plane))
-        if a in ((0, 0), (0, 1), (0, 3)):
+        if a in ((0, 1), (0, 3)):
             add(a, (3, a[1]))
-        if a == (1, 2):
-            add(a, (-2, 2))
+        if a in ((1, 0), (1, 2)):
+            add(a, (-2, a[1]))
     for a in ahead:
         if a[1] == 4:
             add(a, a)

time: 76.1 us -> 76.8 us (level)
  starting transfers between devices: 19.7 us -> 18.5 us
  waiting for transfers between devices: 20.8 us -> 22 us
    ppermute x1, starting transfers between devices: 3.64 us -> 1.92 us  [local(): below = lax.ppermute(below, AXES, shift_perm(-1, 0))]
    ppermute x1, waiting for transfers between devices: 4.65 us -> 5.86 us  [local(): ahead = lax.ppermute(ahead, AXES, shift_perm(0, 1))]
where the time goes in v8:
time: 76.8 us; the launch traced here: 76.5 us
  blocking collectives  25.4 us (33%)
  waiting for transfers between devices  22 us (29%)
  starting transfers between devices  18.5 us (24%)
  Pallas kernels  7.7 us (10%)
  between operations  1.4 us (2%)
  other arithmetic  0.79 us (1%)
    all_to_all x1, blocking collectives, local(): lax.all_to_all(partial, AXES, split_axis=0, concat_axis=0, tiled=True)  25.4 us
    all_to_all x1, waiting for transfers between devices, local(): lax.all_to_all(send.reshape(16 * SENT, 1, 128), 'trial', split_axis=0, co...  14.9 us
    all_to_all x1, starting transfers between devices, local(): lax.all_to_all(send.reshape(16 * SENT, 1, 128), 'trial', split_axis=0, co...  9.99 us
    ppermute x1, waiting for transfers between devices, local(): ahead = lax.ppermute(ahead, AXES, shift_perm(0, 1))  5.86 us
    pallas_call x3, Pallas kernels, local(): pl.pallas_call(functools.partial(kernel, stage), out_shape=shapes, in_spe...  4.58 us
    pallas_call x1, Pallas kernels, local(): pl.pallas_call(pack_kernel, out_shape=[shape(16 * SENT, ()), shape(8, ())...  2.95 us
    ppermute x1, starting transfers between devices, local(): theirs = lax.ppermute(scalars, 'freq', [(0, 1), (1, 0)])  2.85 us
    ppermute x1, starting transfers between devices, local(): above = lax.ppermute(above, AXES, shift_perm(1, 0))  2.43 us
  transfers between devices with their start and end apart: 5, of which 3 were waited for; matrix products, arithmetic and copies ran while one was open for 0% of the time, Pallas kernels for 4%

profile of v8, /device:TPU:1, one launch (start us, length us, event | category | flops | bytes accessed | tf_op | source)
XLA Modules:
  0.0 76.5 jit_solution(12278916672625727913)
XLA Ops:
  1.3 3.0 %shard_map.73 = (f32[1184,128]{1,0:T(8,128)}, f32[8,128]{1,0:T(8,128)}) custom-call(f32[1]{0:T(128)S(6)} %copy.10.energy, f32[1,4]{1,0:T(1,128)} %cheb.1, f32[1]{0:T(128)S(6)} %copy.11.shift, f32[32,64,128]{2,1,0:T(8,128)} %bitcast.14, f32[4,64,128]{2,1,0:T(8,128)} %bitcast.16, f32[4,64,128]{2,1,0:T(8,128)} %potential_hbm.1), custom_call_target="tpu_custom_call" | custom-call | tf_op jit(solution)/shard_map/pallas_call | solution.py:366
  4.3 0.0 copy-start
  4.3 10.0 %all-to-all-start = ((f32[1184,1,128]{2,1,0:T(1,128)}), f32[1184,1,128]{2,1,0:T(1,128)S(1)}, u32[]{:S(2)}, u32[]{:S(2)}) async-start(f32[1184,1,128]{2,1,0:T(1,128)} %bitcast.15), calls=%async_computation | async-start | bytes 1212416 | tf_op jit(solution)/shard_map/all_to_all | solution.py:379
  14.3 0.0 copy-done
  14.3 2.9 %collective-permute-start = (f32[8,128]{1,0:T(8,128)S(1)}, f32[8,128]{1,0:T(8,128)S(1)}, u32[]{:S(2)}, u32[]{:S(2)}) collective-permute-start(f32[8,128]{1,0:T(8,128)S(1)} %copy-done), channel_id=1, source_target_pairs={{0,1},{1,0},{2,3},{3,2},{4,5},{5,4},{6,7},{7,6},{8,9},{9,8},{10,11... | collective-permute-start | bytes 12296 | tf_op jit(solution)/shard_map/ppermute | solution.py:381
  17.1 1.2 %collective-permute-done.theirs = f32[8,128]{1,0:T(8,128)S(1)} collective-permute-done((f32[8,128]{1,0:T(8,128)S(1)}, f32[8,128]{1,0:T(8,128)S(1)}, u32[]{:S(2)}, u32[]{:S(2)}) %collective-permute-start) | collective-permute-done | bytes 4128 | tf_op jit(solution)/shard_map/ppermute | solution.py:381
  18.3 14.9 %all-to-all-done = f32[1184,1,128]{2,1,0:T(1,128)S(1)} async-done(((f32[1184,1,128]{2,1,0:T(1,128)}), f32[1184,1,128]{2,1,0:T(1,128)S(1)}, u32[]{:S(2)}, u32[]{:S(2)}) %all-to-all-start) | async-done | bytes 606240 | tf_op jit(solution)/shard_map/all_to_all | solution.py:379
  33.3 0.2 shard_map.74
  33.5 1.3 %collective-permute-start.1 = (f32[16,56,128]{2,1,0:T(8,128)S(1)}, f32[16,56,128]{2,1,0:T(8,128)S(1)}, u32[]{:S(2)}, u32[]{:S(2)}) collective-permute-start(f32[16,56,128]{2,1,0:T(8,128)S(1)} %get-tuple-element.19), channel_id=1, source_target_pairs={{3,0},{5,3},{6,5},{8,6},{11,8},{13,11},{14,13},{19,16},{21,19},{22... | collective-permute-start | bytes 1376264 | tf_op jit(solution)/shard_map/ppermute | solution.py:391
  34.8 1.9 %collective-permute-start.3 = (f32[16,64,128]{2,1,0:T(8,128)S(1)}, f32[16,64,128]{2,1,0:T(8,128)S(1)}, u32[]{:S(2)}, u32[]{:S(2)}) collective-permute-start(f32[16,64,128]{2,1,0:T(8,128)S(1)} %get-tuple-element.22), channel_id=1, source_target_pairs={{0,16},{3,19},{5,21},{6,22},{8,24},{11,27},{13,29},{14,30},{16,32}... | collective-permute-start | bytes 1572872 | tf_op jit(solution)/shard_map/ppermute | solution.py:393
  36.7 2.4 %collective-permute-start.2 = (f32[16,56,128]{2,1,0:T(8,128)S(1)}, f32[16,56,128]{2,1,0:T(8,128)S(1)}, u32[]{:S(2)}, u32[]{:S(2)}) collective-permute-start(f32[16,56,128]{2,1,0:T(8,128)S(1)} %get-tuple-element.21), channel_id=1, source_target_pairs={{16,0},{19,3},{21,5},{22,6},{24,8},{27,11},{29,13},{30,14},{32,16}... | collective-permute-start | bytes 1376264 | tf_op jit(solution)/shard_map/ppermute | solution.py:392
  39.1 0.0 copy-start.1
  39.1 0.6 copy-done.1
  39.8 2.2 %shard_map.75 = (f32[128,128]{1,0:T(8,128)S(1)}, f32[128,128]{1,0:T(8,128)S(1)}) custom-call(f32[8,128]{1,0:T(8,128)S(1)} %get-tuple-element.16.args_0_, s32[1,128]{1,0:T(1,128)S(1)} %bitcast.13, f32[16,80,128]{2,1,0:T(8,128)S(1)} %get-tuple-element.17.args_2_.args_3_), custom_call_target="tpu_custom_call" | custom-call | flops 2000000000 | bytes 3145728 | tf_op jit(solution)/shard_map/pallas_call | solution.py:405
  42.0 5.9 %collective-permute-done.1.args_3_.args_4_ = f32[16,56,128]{2,1,0:T(8,128)S(1)} collective-permute-done((f32[16,56,128]{2,1,0:T(8,128)S(1)}, f32[16,56,128]{2,1,0:T(8,128)S(1)}, u32[]{:S(2)}, u32[]{:S(2)}) %collective-permute-start.1) | collective-permute-done | bytes 458784 | tf_op jit(solution)/shard_map/ppermute | solution.py:391
  47.8 0.7 shard_map.76.args_1_
  48.6 0.0 collective-permute-done.2.args_5_
  48.6 0.0 collective-permute-done.3.args_6_
  48.6 1.7 %shard_map.77 = f32[256,128]{1,0:T(8,128)S(1)} custom-call(f32[8,128]{1,0:T(8,128)S(1)} %get-tuple-element.16.args_0_, f32[128,128]{1,0:T(8,128)S(1)} %shard_map.76.args_1_, f32[128,128]{1,0:T(8,128)S(1)} %get-tuple-element.20.args_2_, f32[16,80,128]{2,1,0:T(8,128)S(1)} %get-tuple-element.17.args_2_.args_3_, ...), custom_call_target="tpu_custom_call" | custom-call | flops 2000000000 | bytes 3145728 | tf_op jit(solution)/shard_map/pallas_call | solution.py:405
  50.3 25.4 %all_to_all.14 = f32[256,1,128]{2,1,0:T(1,128)S(1)} all-to-all(f32[256,1,128]{2,1,0:T(1,128)S(1)} %bitcast.12), channel_id=1, replica_groups=mesh['trial'=16,'slab'=8,'freq'=2] {'trial','slab','freq'}, dimensions={0} | all-to-all | bytes 262144 | tf_op jit(solution)/shard_map/all_to_all | solution.py:414
  75.7 0.8 %reduce_sum.9 = f32[128]{0:T(128)} reduce(f32[256,1,128]{2,1,0:T(1,128)S(1)} %all_to_all.14, f32[]{:T(128)} %constant.0.clone.1), dimensions={0,1}, to_apply=%region_0.0 | reduce | flops 32640 | bytes 131588 | tf_op jit(solution)/shard_map/reduce_sum | solution.py:415
Async XLA Ops:
  4.3 10.0 %copy-start = (f32[8,128]{1,0:T(8,128)S(1)}, f32[8,128]{1,0:T(8,128)}, u32[]{:S(2)}) copy-start(f32[8,128]{1,0:T(8,128)} %get-tuple-element.15.ours) | copy-start | bytes 12292
  4.3 29.0 %all-to-all-start = ((f32[1184,1,128]{2,1,0:T(1,128)}), f32[1184,1,128]{2,1,0:T(1,128)S(1)}, u32[]{:S(2)}, u32[]{:S(2)}) async-start(f32[1184,1,128]{2,1,0:T(1,128)} %bitcast.15), calls=%async_computation | async-start | bytes 1212416 | tf_op jit(solution)/shard_map/all_to_all | solution.py:379
  14.3 4.1 %collective-permute-start = (f32[8,128]{1,0:T(8,128)S(1)}, f32[8,128]{1,0:T(8,128)S(1)}, u32[]{:S(2)}, u32[]{:S(2)}) collective-permute-start(f32[8,128]{1,0:T(8,128)S(1)} %copy-done), channel_id=1, source_target_pairs={{0,1},{1,0},{2,3},{3,2},{4,5},{5,4},{6,7},{7,6},{8,9},{9,8},{10,11... | collective-permute-start | bytes 12296 | tf_op jit(solution)/shard_map/ppermute | solution.py:381
  33.5 14.4 %collective-permute-start.1 = (f32[16,56,128]{2,1,0:T(8,128)S(1)}, f32[16,56,128]{2,1,0:T(8,128)S(1)}, u32[]{:S(2)}, u32[]{:S(2)}) collective-permute-start(f32[16,56,128]{2,1,0:T(8,128)S(1)} %get-tuple-element.19), channel_id=1, source_target_pairs={{3,0},{5,3},{6,5},{8,6},{11,8},{13,11},{14,13},{19,16},{21,19},{22... | collective-permute-start | bytes 1376264 | tf_op jit(solution)/shard_map/ppermute | solution.py:391
  34.8 13.8 %collective-permute-start.3 = (f32[16,64,128]{2,1,0:T(8,128)S(1)}, f32[16,64,128]{2,1,0:T(8,128)S(1)}, u32[]{:S(2)}, u32[]{:S(2)}) collective-permute-start(f32[16,64,128]{2,1,0:T(8,128)S(1)} %get-tuple-element.22), channel_id=1, source_target_pairs={{0,16},{3,19},{5,21},{6,22},{8,24},{11,27},{13,29},{14,30},{16,32}... | collective-permute-start | bytes 1572872 | tf_op jit(solution)/shard_map/ppermute | solution.py:393
  36.7 11.9 %collective-permute-start.2 = (f32[16,56,128]{2,1,0:T(8,128)S(1)}, f32[16,56,128]{2,1,0:T(8,128)S(1)}, u32[]{:S(2)}, u32[]{:S(2)}) collective-permute-start(f32[16,56,128]{2,1,0:T(8,128)S(1)} %get-tuple-element.21), channel_id=1, source_target_pairs={{16,0},{19,3},{21,5},{22,6},{24,8},{27,11},{29,13},{30,14},{32,16}... | collective-permute-start | bytes 1376264 | tf_op jit(solution)/shard_map/ppermute | solution.py:392
  39.1 0.7 copy-start.1
